TPU v7x, 256 devices: a whole 4x4x8 slice. The times are simulated.
256 devices in a mesh: tok: 64 (over x, z_lo, y), proj: 4 (over z_hi, core).
Axes of the slice: x: 4, y: 4, z: 8 (z_hi: 2, z_lo: 4; z = z_hi * 4 + z_lo), core: 2. Of those that a mesh axis runs over, the one named last changes fastest.
Arguments:
- latent: bfloat16 [65536, 512], P('tok', 'proj'), may hold values from -400 to 400
- grad_key: bfloat16 [65536, 2048], P('tok', 'proj'), may hold values from -400 to 400
- grad_value: bfloat16 [65536, 2048], P('tok', 'proj'), may hold values from -400 to 400
Outputs:
- latent_cov: float32 [512, 512], P(None, 'proj')
- key_cov: float32 [2048, 2048], P('tok', 'proj')
- value_cov: float32 [2048, 2048], P('tok', 'proj')
All inputs are finite; a program needn't handle non-finite values.
Results may differ from a plain program's by a relative error of at most 0.0003.
Values may be sent and summed in bfloat16 or wider, within the bound.
No kernel may reach another device: no remote copies, remote signals or barrier semaphores. Data moves between devices by JAX's collectives and lax.ppermute only.
A program may use at most 64 MiB of HBM per device.

v0:
```python
import functools
import itertools

import jax
import jax.numpy as jnp
from jax import lax
from jax.experimental import pallas as pl
from jax.experimental.pallas import tpu as pltpu
from jax.sharding import Mesh, PartitionSpec as P

AXES = ("x", "zl", "y", "zh", "core")
SIZES = (4, 4, 4, 2, 2)
CHUNKS = (1, 3)
F32 = jnp.float32


def move(values, where):
    pairs = []
    for source, place in enumerate(itertools.product(*[range(n) for n in SIZES])):
        target = where(*place)
        if target is None:
            continue
        index = 0
        for n, t in zip(SIZES, target):
            index = index * n + t % n
        pairs.append((source, index))
    return lax.ppermute(values, AXES, pairs)


def to_core(x, zl, y, zh, core):
    return (x, zl, y, zh, 1 - core)


def to_half(x, zl, y, zh, core):
    return (x, zl, y, 1 - zh, core)


def first(step):
    return lambda x, zl, y, zh, core: (
        (x + step, zl, y, zh, core) if core == 0 else (x, zl, y + step, zh, core)
    )


def second(step):
    return lambda x, zl, y, zh, core: (
        (x, zl, y + step, zh, core) if core == 0 else (x + step, zl, y, zh, core)
    )


def along_z(step):
    return lambda x, zl, y, zh, core: (x, zl + step, y, zh, core)


def homeward(x, zl, y, zh, core):
    return (x, zl, y, 1 - zh, core) if x // 2 == zh else (x + 2, zl, y, zh, core)


def sideways(x, zl, y, zh, core):
    return (x ^ 1, zl, y, zh, 1 - core) if x // 2 != zh and x % 2 != core else None


def product(left, right):
    return lax.dot_general(left, right, (((0,), (0,)), ((), ())), preferred_element_type=F32)


def block_of(kind, zh, core):
    half = zh if kind < 2 else 1 - zh
    return 2 * half + (core if kind % 2 == 0 else 1 - core)


def place(scalars, kind, zl, yb):
    x, y, zh, core = scalars[0], scalars[1], scalars[3], scalars[4]
    jx = lax.rem(block_of(kind, zh, core) - x + 4, 4)
    jy = lax.rem(yb - y + 4, 4)
    is0 = core == 0
    return (
        jnp.where(is0, jx, jy),
        jnp.where(is0, 4 * zl + yb, 4 * kind + zl),
    )


def rows_at(index, size, offset, count):
    return pl.ds(pl.multiple_of(index * size + offset, 8), count)


def emit(room, outs, sems):
    copies = [pltpu.make_async_copy(room.at[j], outs[j], sems.at[j]) for j in range(4)]
    for c in copies:
        c.start()
    for c in copies:
        c.wait()


def own_kernel(scalars, km, ko, vm, vo, *rest):
    outs, room, sems = rest[:4], rest[4], rest[5]
    for kind, (left, right) in enumerate([(km, km), (ko, km), (vm, vm), (vo, vm)]):
        for zl in range(4):
            block = product(left[:, 128 * zl : 128 * (zl + 1)], right[...])
            for yb in range(4):
                part, i = place(scalars, kind, zl, yb)
                for cg in range(4):
                    room[part, rows_at(i, 128, 32 * cg, 32), :] = block[
                        32 * yb : 32 * (yb + 1), 128 * cg : 128 * (cg + 1)
                    ]
    emit(room, outs, sems)


def cross_kernel(latent, scalars, nm, no, *rest):
    fars, outs, room, sems = rest[:-6], rest[-6:-2], rest[-2], rest[-1]
    size, e = room.shape[1] // 16, 0
    if latent:
        lefts, fars = fars[:4], fars[4:]
        for kind, left in enumerate(lefts):
            block = product(left[...], lefts[0][...])
            for zl in range(4):
                for yb in range(4):
                    part, i = place(scalars, kind, zl, yb)
                    row = 32 * zl + 8 * yb
                    room[part, rows_at(i, size, size - 8, 8), :] = block[row : row + 8, :]
    for far in fars:
        quarters = far.shape[1] // 128
        for kind, near in enumerate([nm, no]):
            for zl in range(4):
                block = product(near[:, 128 * zl : 128 * (zl + 1)], far[...])
                for yb in range(4):
                    part, i = place(scalars, kind, zl, yb)
                    for q in range(quarters):
                        room[part, rows_at(i, size, 32 * (e + q), 32), :] = block[
                            32 * yb : 32 * (yb + 1), 128 * q : 128 * (q + 1)
                        ]
            for q in range(quarters):
                block = product(far[:, 128 * q : 128 * (q + 1)], near[...])
                for zl in range(4):
                    for yb in range(4):
                        part, i = place(scalars, kind + 2, zl, yb)
                        row = 32 * zl + 8 * yb
                        for cg in range(4):
                            at = 32 * (e + q) + 8 * cg
                            room[part, rows_at(i, size, at, 8), :] = block[
                                row : row + 8, 128 * cg : 128 * (cg + 1)
                            ]
        e += quarters
    emit(room, outs, sems)


def middle_kernel(sizes, gathered, scalars, *refs):
    x, y, zh, core = scalars[0], scalars[1], scalars[3], scalars[4]
    ins, outs = refs[:-4], refs[-4:]
    if gathered:
        piece, ins = ins[-1], ins[:-1]
    each = len(ins) // len(sizes)
    is0 = core == 0
    whole = sum(sizes)
    for j, out in enumerate(outs):
        yb = lax.rem(y + j, 4)
        xb = lax.rem(x + j, 4)
        kind = 2 * jnp.where(xb // 2 == zh, 0, 1) + jnp.where(xb % 2 == core, 0, 1)
        for slab in range(4):
            index = jnp.where(is0, 4 * slab + yb, 4 * kind + slab)
            start = whole * slab
            for n, size in enumerate(sizes):
                at = rows_at(index, size, 0, size)
                total = ins[each * n][at]
                for r in ins[each * n + 1 : each * (n + 1)]:
                    total += r[at]
                out[start : start + size] = total
                start += size
        if gathered:
            out[4 * whole : 4 * whole + 8] = piece[...]


def last_kernel(size, gathered, scalars, a, b, c, d, *outs):
    zl = scalars[2]
    for j, out in enumerate(outs):
        at = rows_at(lax.rem(zl + j, 4), size, 0, size)
        out[:size] = (a[at] + b[at]) + (c[at] + d[at])
        if gathered:
            for n, r in enumerate((a, b, c, d)):
                out[size + 8 * n : size + 8 * (n + 1)] = r[4 * size : 4 * size + 8]


def latent_kernel(scale, scalars, a, b, c, d, out):
    x, y, zl, core = scalars[0], scalars[1], scalars[2], scalars[4]
    is0 = core == 0
    for j1, ref in enumerate((a, b, c, d)):
        for jz in range(4):
            for j2 in range(4):
                xb = lax.rem(x + 4 - jnp.where(is0, j1, j2), 4)
                yb = lax.rem(y + 4 - jnp.where(is0, j2, j1), 4)
                zb = lax.rem(zl + 4 - jz, 4)
                to = rows_at(16 * xb + 4 * zb + yb, 8, 0, 8)
                at = 32 * jz + 8 * j2
                out[to, :] = ref[at : at + 8, :] * scale


def finish_kernel(scale, scalars, own, cross, moved, turned, order, key_out, value_out):
    x, zh, core = scalars[0], scalars[3], scalars[4]
    inside = x // 2 == zh

    @pl.when(inside)
    def _():
        for cg in range(4):
            key_out[:, 128 * cg : 128 * (cg + 1)] = own[32 * cg : 32 * (cg + 1)] * scale
            value_out[:, 128 * cg : 128 * (cg + 1)] = moved[32 * cg : 32 * (cg + 1)] * scale

    @pl.when(jnp.logical_not(inside))
    def _():
        back = jnp.zeros(key_out.shape, F32)
        for e in range(4):
            rest = moved[32 * e : 32 * (e + 1)] * scale
            for _ in range(3):
                top = rest.astype(jnp.bfloat16)
                back += jnp.dot(top, order[128 * e : 128 * (e + 1)], preferred_element_type=F32)
                rest -= top.astype(F32)

        here = lax.rem(x, 2) == core

        def stay_to(out):
            for e in range(4):
                for cg in range(4):
                    at = 32 * e + 8 * cg
                    tile = jnp.where(here, cross[at : at + 8], turned[at : at + 8])
                    out[8 * e : 8 * (e + 1), 128 * cg : 128 * (cg + 1)] = tile * scale

        @pl.when(zh == 0)
        def _():
            stay_to(key_out)
            value_out[...] = back

        @pl.when(zh == 1)
        def _():
            key_out[...] = back
            stay_to(value_out)


SMEM = pl.BlockSpec(memory_space=pltpu.SMEM)
VMEM = pl.BlockSpec(memory_space=pltpu.VMEM)
ANY = pl.BlockSpec(memory_space=pl.ANY)
LIMIT = pltpu.CompilerParams(vmem_limit_bytes=40 * 2**20)


def blocks_call(kernel, rows, scalars, *operands):
    outs = [jax.ShapeDtypeStruct((rows, 128), F32)] * 4
    return pl.pallas_call(
        kernel,
        out_shape=outs,
        in_specs=[SMEM] + [VMEM] * len(operands),
        out_specs=[ANY] * len(outs),
        scratch_shapes=[pltpu.VMEM((4, rows, 128), F32), pltpu.SemaphoreType.DMA((len(outs),))],
        compiler_params=LIMIT,
        cost_estimate=pl.CostEstimate(flops=0, bytes_accessed=0, transcendentals=0),
    )(scalars, *operands)


def sums_call(kernel, shapes, scalars, *operands):
    outs = [jax.ShapeDtypeStruct(s, F32) for s in shapes]
    head = [] if scalars is None else [scalars]
    return pl.pallas_call(
        kernel,
        out_shape=outs,
        in_specs=[SMEM] * len(head) + [VMEM] * len(operands),
        out_specs=[VMEM] * len(outs),
        compiler_params=LIMIT,
        cost_estimate=pl.CostEstimate(flops=0, bytes_accessed=0, transcendentals=0),
    )(*head, *operands)


def exchange(parts, direction):
    return [parts[0]] + [move(parts[j], direction(j)) for j in (1, 2, 3)]


def after(value, *others):
    return lax.optimization_barrier((value,) + others)[0]


def shards(latent, grad_key, grad_value):
    x, zl, y, zh, core = (lax.axis_index(a) for a in AXES)
    scalars = jnp.stack([x, y, zl, zh, core]).astype(jnp.int32)
    scale = 1.0 / (latent.shape[0] * 64)
    width = grad_key.shape[1]
    low = zh == 0

    to = jnp.arange(width)
    source = 128 * ((to // 32) % 4) + 32 * ((to // 8) % 4) + 8 * (to // 128) + to % 8
    order = (source[:, None] == jnp.arange(width)[None, :]).astype(jnp.bfloat16)
    chosen = jnp.where(low, grad_value, grad_key)
    ordered, start = [], 0
    for quarters in CHUNKS:
        pick = (jnp.arange(width)[:, None] == source[None, start : start + 128 * quarters])
        part = jnp.dot(chosen, pick.astype(jnp.bfloat16), preferred_element_type=F32)
        ordered.append(part.astype(jnp.bfloat16))
        start += 128 * quarters
    latent_far = move(latent, to_half)
    far0 = move(ordered[0], to_half)
    far1 = move(ordered[1], to_half)

    key_other = move(grad_key, to_core)
    value_other = move(grad_value, to_core)
    latent_other = move(latent, to_core)
    near = jnp.where(low, grad_key, grad_value)
    near_other = jnp.where(low, key_other, value_other)

    def middle(sizes, *parts, gathered=False, gate):
        shape = (4 * sum(sizes) + (8 if gathered else 0), 128)
        kernel = functools.partial(middle_kernel, sizes, gathered)
        return sums_call(kernel, [shape] * 4, after(scalars, gate), *parts)

    def last(size, *parts, gathered=False, gate=()):
        shape = (size + (32 if gathered else 0), 128)
        kernel = functools.partial(last_kernel, size, gathered)
        return sums_call(kernel, [shape] * 4, after(scalars, gate), *parts)

    own = blocks_call(
        own_kernel, 16 * 128, scalars, grad_key, key_other, grad_value, value_other
    )
    gate = own[0]
    own = exchange(own, first)

    latent_far_other = move(latent_far, to_core)
    c0 = blocks_call(
        functools.partial(cross_kernel, True), 16 * 40, after(scalars, gate), near, near_other,
        latent, latent_other, latent_far, latent_far_other, far0,
    )
    c1 = blocks_call(
        functools.partial(cross_kernel, False), 16 * 96, after(scalars, c0[0]), near, near_other, far1
    )
    c0 = exchange(c0, first)
    c0 = middle((128, 40), *own, *c0, gate=c1[0])
    c1 = exchange(c1, first)
    c0 = exchange(c0, second)
    c0 = exchange(last(168, *c0), along_z)
    c0 = (c0[0] + c0[1]) + (c0[2] + c0[3])
    own = c0[:128]
    c = middle((96,), *c1, c0[160:], gathered=True, gate=c0)
    c = exchange(c, second)
    c = exchange(last(96, *c, gathered=True), along_z)
    pieces = jnp.concatenate([part[96:] for part in c], axis=0)
    ends = (c[0][:96] + c[1][:96]) + (c[2][:96] + c[3][:96])
    crossed = jnp.concatenate([c0[128:160], ends], axis=0)
    moved = move(jnp.where(x // 2 == zh, crossed, own), homeward)
    turned = move(crossed, sideways)
    (latent_sum,) = sums_call(
        functools.partial(latent_kernel, scale), [(512, 128)], scalars, *exchange([pieces] * 4, first)
    )
    key_sum, value_sum = sums_call(
        functools.partial(finish_kernel, scale), [(32, width)] * 2, scalars, own, crossed, moved, turned, order
    )
    return latent_sum, key_sum, value_sum


def solution(mesh):
    fine = Mesh(mesh.devices.reshape(SIZES), AXES)
    tok, proj = ("x", "zl", "y"), ("zh", "core")
    placed = (P(tok, proj), P(tok, proj), P(tok, proj))
    return jax.shard_map(
        shards,
        mesh=fine,
        in_specs=placed,
        out_specs=(P(None, proj), P(tok, proj), P(tok, proj)),
        check_vma=False,
    )
```

profile of v0, /device:TPU:32, one launch (start us, length us, event | category | flops | bytes accessed | tf_op | source)
XLA Modules:
  0.0 149.8 jit_solution(18246401769326953313)
XLA Ops:
  1.2 6.3 %collective-permute-start.3 = (bf16[1024,128]{1,0:T(8,128)(2,1)}, bf16[1024,128]{1,0:T(8,128)(2,1)S(1)}, u32[]{:S(2)}, u32[]{:S(2)}) collective-permute-start(bf16[1024,128]{1,0:T(8,128)(2,1)} %rest_0_.1), channel_id=1, source_target_pairs={{0,2},{1,3},{2,0},{3,1},{4,6},{5,7},{6,4},{7,5},{8,10},{9,11},{10,... | collective-permute-start | bytes 786440 | tf_op jit(solution)/shard_map/ppermute | solution.py:27
  7.6 2.5 %convolution_convert_fusion.1 = bf16[1024,128]{1,0:T(8,128)(2,1)} fusion(bf16[1024,512]{1,0:T(8,128)(2,1)} %vm.1, bf16[1024,512]{1,0:T(8,128)(2,1)} %km.1, pred[]{:T(512)S(6)} %eq.49, s32[128]{0:T(128)S(1)} %slice.39), kind=kOutput, calls=%fused_computation.1 | convolution fusion | flops 134938624 | bytes 2359809 | tf_op jit(solution)/shard_map/dot_general | solution.py:290
  11.0 5.9 %collective-permute-start.6 = (bf16[1024,384]{1,0:T(8,128)(2,1)S(1)}, bf16[1024,384]{1,0:T(8,128)(2,1)S(1)}, u32[]{:S(2)}, u32[]{:S(2)}) collective-permute-start(bf16[1024,384]{1,0:T(8,128)(2,1)S(1)} %convolution_convert_fusion), channel_id=1, source_target_pairs={{0,2},{1,3},{2,0},{3,1},{4,6},{5,7},{6,4},{7,5},{8,10},{9,11},{10,... | collective-permute-start | bytes 2359304 | tf_op jit(solution)/shard_map/ppermute | solution.py:27
  17.0 3.9 %shard_map.58 = (f32[2048,128]{1,0:T(8,128)S(1)}, f32[2048,128]{1,0:T(8,128)S(1)}, f32[2048,128]{1,0:T(8,128)S(1)}, f32[2048,128]{1,0:T(8,128)S(1)}) custom-call(s32[5]{0:T(128)S(1)} %stack.23.scalars, bf16[1024,512]{1,0:T(8,128)(2,1)S(1)} %copy-done, bf16[1024,512]{1,0:T(8,128)(2,1)S(1)} %collective-permute-done.ko, bf16[1024,512]{1,0:T(8,128)(2,1)S(1)} %copy-done.1, ...), custom_call_target="tpu_custom_call" | custom-call | tf_op jit(solution)/shard_map/pallas_call | solution.py:244
  20.9 1.6 %collective-permute-start.7 = (f32[2048,128]{1,0:T(8,128)S(1)}, f32[2048,128]{1,0:T(8,128)S(1)}, u32[]{:S(2)}, u32[]{:S(2)}) collective-permute-start(f32[2048,128]{1,0:T(8,128)S(1)} %get-tuple-element.43), channel_id=1, source_target_pairs={{0,64},{1,5},{2,66},{3,7},{4,68},{5,9},{6,70},{7,11},{8,72},{9,13}... | collective-permute-start | bytes 3145736 | tf_op jit(solution)/shard_map/ppermute | solution.py:27
  22.5 13.6 %collective-permute-done.5.rest_4_ = bf16[1024,128]{1,0:T(8,128)(2,1)} collective-permute-done((bf16[1024,128]{1,0:T(8,128)(2,1)}, bf16[1024,128]{1,0:T(8,128)(2,1)}, u32[]{:S(2)}, u32[]{:S(2)}) %collective-permute-start.5) | collective-permute-done | bytes 262176 | tf_op jit(solution)/shard_map/ppermute | solution.py:27
  36.1 3.0 %collective-permute-start.8 = (f32[2048,128]{1,0:T(8,128)S(1)}, f32[2048,128]{1,0:T(8,128)S(1)}, u32[]{:S(2)}, u32[]{:S(2)}) collective-permute-start(f32[2048,128]{1,0:T(8,128)S(1)} %get-tuple-element.44), channel_id=1, source_target_pairs={{0,128},{1,9},{2,130},{3,11},{4,132},{5,13},{6,134},{7,15},{8,136}... | collective-permute-start | bytes 3145736 | tf_op jit(solution)/shard_map/ppermute | solution.py:27
  42.0 2.9 %shard_map.59 = (f32[640,128]{1,0:T(8,128)S(1)}, f32[640,128]{1,0:T(8,128)S(1)}, f32[640,128]{1,0:T(8,128)S(1)}, f32[640,128]{1,0:T(8,128)S(1)}) custom-call(s32[5]{0:T(128)S(1)} %stack.23.scalars, bf16[1024,512]{1,0:T(8,128)(2,1)S(1)} %broadcast_select_fusion.2.nm, bf16[1024,512]{1,0:T(8,128)(2,1)S(1)} %broadcast_select_fusion.1.no, ...), custom_call_target="tpu_custom_call" | custom-call | tf_op jit(solution)/shard_map/pallas_call | solution.py:244
  45.9 19.3 %collective-permute-done.6.rest_0_ = bf16[1024,384]{1,0:T(8,128)(2,1)S(1)} collective-permute-done((bf16[1024,384]{1,0:T(8,128)(2,1)S(1)}, bf16[1024,384]{1,0:T(8,128)(2,1)S(1)}, u32[]{:S(2)}, u32[]{:S(2)}) %collective-permute-start.6) | collective-permute-done | bytes 786464 | tf_op jit(solution)/shard_map/ppermute | solution.py:27
  65.2 3.0 %collective-permute-start.11 = (f32[640,128]{1,0:T(8,128)S(1)}, f32[640,128]{1,0:T(8,128)S(1)}, u32[]{:S(2)}, u32[]{:S(2)}) collective-permute-start(f32[640,128]{1,0:T(8,128)S(1)} %get-tuple-element.47), channel_id=1, source_target_pairs={{0,128},{1,9},{2,130},{3,11},{4,132},{5,13},{6,134},{7,15},{8,136}... | collective-permute-start | bytes 983048 | tf_op jit(solution)/shard_map/ppermute | solution.py:27
  69.4 2.9 %shard_map.60 = (f32[1536,128]{1,0:T(8,128)S(1)}, f32[1536,128]{1,0:T(8,128)S(1)}, f32[1536,128]{1,0:T(8,128)S(1)}, f32[1536,128]{1,0:T(8,128)S(1)}) custom-call(s32[5]{0:T(128)S(1)} %stack.23.scalars, bf16[1024,512]{1,0:T(8,128)(2,1)S(1)} %broadcast_select_fusion.2.nm, bf16[1024,512]{1,0:T(8,128)(2,1)S(1)} %broadcast_select_fusion.1.no, ...), custom_call_target="tpu_custom_call" | custom-call | tf_op jit(solution)/shard_map/pallas_call | solution.py:244
  72.3 1.5 collective-permute-done.11.refs_6_
  73.8 3.6 %collective-permute-done.12.refs_7_ = f32[640,128]{1,0:T(8,128)S(1)} collective-permute-done((f32[640,128]{1,0:T(8,128)S(1)}, f32[640,128]{1,0:T(8,128)S(1)}, u32[]{:S(2)}, u32[]{:S(2)}) %collective-permute-start.12) | collective-permute-done | bytes 327712 | tf_op jit(solution)/shard_map/ppermute | solution.py:27
  78.3 1.7 %collective-permute-start.13 = (f32[672,128]{1,0:T(8,128)S(1)}, f32[672,128]{1,0:T(8,128)S(1)}, u32[]{:S(2)}, u32[]{:S(2)}) collective-permute-start(f32[672,128]{1,0:T(8,128)S(1)} %get-tuple-element.50), channel_id=1, source_target_pairs={{0,4},{1,65},{2,6},{3,67},{4,8},{5,69},{6,10},{7,71},{8,12},{9,73}... | collective-permute-start | bytes 1032200 | tf_op jit(solution)/shard_map/ppermute | solution.py:27
  81.3 2.7 %collective-permute-start.20 = (f32[1536,128]{1,0:T(8,128)S(1)}, f32[1536,128]{1,0:T(8,128)S(1)}, u32[]{:S(2)}, u32[]{:S(2)}) collective-permute-start(f32[1536,128]{1,0:T(8,128)S(1)} %get-tuple-element.59), channel_id=1, source_target_pairs={{0,128},{1,9},{2,130},{3,11},{4,132},{5,13},{6,134},{7,15},{8,136}... | collective-permute-start | bytes 2359304 | tf_op jit(solution)/shard_map/ppermute | solution.py:27
  84.6 2.9 %collective-permute-start.14 = (f32[672,128]{1,0:T(8,128)S(1)}, f32[672,128]{1,0:T(8,128)S(1)}, u32[]{:S(2)}, u32[]{:S(2)}) collective-permute-start(f32[672,128]{1,0:T(8,128)S(1)} %get-tuple-element.51), channel_id=1, source_target_pairs={{0,8},{1,129},{2,10},{3,131},{4,12},{5,133},{6,14},{7,135},{8,0},{... | collective-permute-start | bytes 1032200 | tf_op jit(solution)/shard_map/ppermute | solution.py:27
  87.5 3.0 %collective-permute-done.13.b = f32[672,128]{1,0:T(8,128)S(1)} collective-permute-done((f32[672,128]{1,0:T(8,128)S(1)}, f32[672,128]{1,0:T(8,128)S(1)}, u32[]{:S(2)}, u32[]{:S(2)}) %collective-permute-start.13) | collective-permute-done | bytes 344096 | tf_op jit(solution)/shard_map/ppermute | solution.py:27
  90.5 1.9 %collective-permute-start.15 = (f32[672,128]{1,0:T(8,128)S(1)}, f32[672,128]{1,0:T(8,128)S(1)}, u32[]{:S(2)}, u32[]{:S(2)}) collective-permute-start(f32[672,128]{1,0:T(8,128)S(1)} %get-tuple-element.52), channel_id=1, source_target_pairs={{0,12},{1,193},{2,14},{3,195},{4,0},{5,197},{6,2},{7,199},{8,4},{9... | collective-permute-start | bytes 1032200 | tf_op jit(solution)/shard_map/ppermute | solution.py:27
  92.4 6.8 %collective-permute-done.14.c = f32[672,128]{1,0:T(8,128)S(1)} collective-permute-done((f32[672,128]{1,0:T(8,128)S(1)}, f32[672,128]{1,0:T(8,128)S(1)}, u32[]{:S(2)}, u32[]{:S(2)}) %collective-permute-start.14) | collective-permute-done | bytes 344096 | tf_op jit(solution)/shard_map/ppermute | solution.py:27
  99.2 4.3 %collective-permute-done.15.d = f32[672,128]{1,0:T(8,128)S(1)} collective-permute-done((f32[672,128]{1,0:T(8,128)S(1)}, f32[672,128]{1,0:T(8,128)S(1)}, u32[]{:S(2)}, u32[]{:S(2)}) %collective-permute-start.15) | collective-permute-done | bytes 344096 | tf_op jit(solution)/shard_map/ppermute | solution.py:27
  104.1 5.3 %collective-permute-start.17 = (f32[168,128]{1,0:T(8,128)S(1)}, f32[168,128]{1,0:T(8,128)S(1)}, u32[]{:S(2)}, u32[]{:S(2)}) collective-permute-start(f32[168,128]{1,0:T(8,128)S(1)} %get-tuple-element.55), channel_id=1, source_target_pairs={{0,32},{1,33},{2,34},{3,35},{4,36},{5,37},{6,38},{7,39},{8,40},{9,... | collective-permute-start | bytes 258056 | tf_op jit(solution)/shard_map/ppermute | solution.py:27
  110.5 3.9 %collective-permute-start.18 = (f32[168,128]{1,0:T(8,128)S(1)}, f32[168,128]{1,0:T(8,128)S(1)}, u32[]{:S(2)}, u32[]{:S(2)}) collective-permute-start(f32[168,128]{1,0:T(8,128)S(1)} %get-tuple-element.56), channel_id=1, source_target_pairs={{0,48},{1,49},{2,50},{3,51},{4,52},{5,53},{6,54},{7,55},{8,56},{9,... | collective-permute-start | bytes 258056 | tf_op jit(solution)/shard_map/ppermute | solution.py:27
  114.7 2.5 %collective-permute-done.18 = f32[168,128]{1,0:T(8,128)S(1)} collective-permute-done((f32[168,128]{1,0:T(8,128)S(1)}, f32[168,128]{1,0:T(8,128)S(1)}, u32[]{:S(2)}, u32[]{:S(2)}) %collective-permute-start.18) | collective-permute-done | bytes 86048 | tf_op jit(solution)/shard_map/ppermute | solution.py:27
  118.3 2.4 %collective-permute-start.23 = (f32[392,128]{1,0:T(8,128)S(1)}, f32[392,128]{1,0:T(8,128)S(1)}, u32[]{:S(2)}, u32[]{:S(2)}) collective-permute-start(f32[392,128]{1,0:T(8,128)S(1)} %get-tuple-element.63), channel_id=1, source_target_pairs={{0,8},{1,129},{2,10},{3,131},{4,12},{5,133},{6,14},{7,135},{8,0},{... | collective-permute-start | bytes 602120 | tf_op jit(solution)/shard_map/ppermute | solution.py:27
  120.7 2.4 %collective-permute-start.24 = (f32[392,128]{1,0:T(8,128)S(1)}, f32[392,128]{1,0:T(8,128)S(1)}, u32[]{:S(2)}, u32[]{:S(2)}) collective-permute-start(f32[392,128]{1,0:T(8,128)S(1)} %get-tuple-element.64), channel_id=1, source_target_pairs={{0,12},{1,193},{2,14},{3,195},{4,0},{5,197},{6,2},{7,199},{8,4},{9... | collective-permute-start | bytes 602120 | tf_op jit(solution)/shard_map/ppermute | solution.py:27
  123.2 4.1 %collective-permute-done.22.b = f32[392,128]{1,0:T(8,128)S(1)} collective-permute-done((f32[392,128]{1,0:T(8,128)S(1)}, f32[392,128]{1,0:T(8,128)S(1)}, u32[]{:S(2)}, u32[]{:S(2)}) %collective-permute-start.22) | collective-permute-done | bytes 200736 | tf_op jit(solution)/shard_map/ppermute | solution.py:27
  129.0 4.0 %collective-permute-start.26 = (f32[128,128]{1,0:T(8,128)S(1)}, f32[128,128]{1,0:T(8,128)S(1)}, u32[]{:S(2)}, u32[]{:S(2)}) collective-permute-start(f32[128,128]{1,0:T(8,128)S(1)} %get-tuple-element.67), channel_id=1, source_target_pairs={{0,32},{1,33},{2,34},{3,35},{4,36},{5,37},{6,38},{7,39},{8,40},{9,... | collective-permute-start | bytes 196616 | tf_op jit(solution)/shard_map/ppermute | solution.py:27
  133.7 2.4 %collective-permute-done.26 = f32[128,128]{1,0:T(8,128)S(1)} collective-permute-done((f32[128,128]{1,0:T(8,128)S(1)}, f32[128,128]{1,0:T(8,128)S(1)}, u32[]{:S(2)}, u32[]{:S(2)}) %collective-permute-start.26) | collective-permute-done | bytes 65568 | tf_op jit(solution)/shard_map/ppermute | solution.py:27
  137.3 1.9 %collective-permute-start.28 = (f32[128,128]{1,0:T(8,128)S(1)}, f32[128,128]{1,0:T(8,128)S(1)}, u32[]{:S(2)}, u32[]{:S(2)}) collective-permute-start(f32[128,128]{1,0:T(8,128)S(1)} %pad_maximum_fusion.a), channel_id=1, source_target_pairs={{0,64},{1,5},{2,66},{3,7},{4,68},{5,9},{6,70},{7,11},{8,72},{9,13}... | collective-permute-start | bytes 196616 | tf_op jit(solution)/shard_map/ppermute | solution.py:27
  139.2 1.8 %collective-permute-start.29 = (f32[128,128]{1,0:T(8,128)S(1)}, f32[128,128]{1,0:T(8,128)S(1)}, u32[]{:S(2)}, u32[]{:S(2)}) collective-permute-start(f32[128,128]{1,0:T(8,128)S(1)} %pad_maximum_fusion.a), channel_id=1, source_target_pairs={{0,128},{1,9},{2,130},{3,11},{4,132},{5,13},{6,134},{7,15},{8,136}... | collective-permute-start | bytes 196616 | tf_op jit(solution)/shard_map/ppermute | solution.py:27
  141.1 1.5 collective-permute-start.30
  142.5 3.7 %collective-permute-start.31 = (f32[128,128]{1,0:T(8,128)S(1)}, f32[128,128]{1,0:T(8,128)S(1)}, u32[]{:S(2)}, u32[]{:S(2)}) collective-permute-start(f32[128,128]{1,0:T(8,128)S(1)} %get-tuple-element.71), channel_id=1, source_target_pairs={{0,2},{1,3},{2,130},{3,131},{4,6},{5,7},{6,134},{7,135},{8,10},{9,... | collective-permute-start | bytes 196616 | tf_op jit(solution)/shard_map/ppermute | solution.py:27
  (68 shorter events, 19.5 us)
Async XLA Ops:
  0.6 10.4 %collective-permute-start = (bf16[1024,512]{1,0:T(8,128)(2,1)}, bf16[1024,512]{1,0:T(8,128)(2,1)S(1)}, u32[]{:S(2)}, u32[]{:S(2)}) collective-permute-start(bf16[1024,512]{1,0:T(8,128)(2,1)} %km.1), channel_id=1, source_target_pairs={{0,1},{1,0},{2,3},{3,2},{4,5},{5,4},{6,7},{7,6},{8,9},{9,8},{10,11... | collective-permute-start | bytes 3145736 | tf_op jit(solution)/shard_map/ppermute | solution.py:27
  0.7 16.3 %collective-permute-start.1 = (bf16[1024,512]{1,0:T(8,128)(2,1)}, bf16[1024,512]{1,0:T(8,128)(2,1)}, u32[]{:S(2)}, u32[]{:S(2)}) collective-permute-start(bf16[1024,512]{1,0:T(8,128)(2,1)} %vm.1), channel_id=1, source_target_pairs={{0,1},{1,0},{2,3},{3,2},{4,5},{5,4},{6,7},{7,6},{8,9},{9,8},{10,11... | collective-permute-start | bytes 3145736 | tf_op jit(solution)/shard_map/ppermute | solution.py:27
  1.2 37.9 %collective-permute-start.3 = (bf16[1024,128]{1,0:T(8,128)(2,1)}, bf16[1024,128]{1,0:T(8,128)(2,1)S(1)}, u32[]{:S(2)}, u32[]{:S(2)}) collective-permute-start(bf16[1024,128]{1,0:T(8,128)(2,1)} %rest_0_.1), channel_id=1, source_target_pairs={{0,2},{1,3},{2,0},{3,1},{4,6},{5,7},{6,4},{7,5},{8,10},{9,11},{10,... | collective-permute-start | bytes 786440 | tf_op jit(solution)/shard_map/ppermute | solution.py:27
  7.5 32.9 %collective-permute-start.2 = (bf16[1024,128]{1,0:T(8,128)(2,1)}, bf16[1024,128]{1,0:T(8,128)(2,1)}, u32[]{:S(2)}, u32[]{:S(2)}) collective-permute-start(bf16[1024,128]{1,0:T(8,128)(2,1)} %rest_0_.1), channel_id=1, source_target_pairs={{0,1},{1,0},{2,3},{3,2},{4,5},{5,4},{6,7},{7,6},{8,9},{9,8},{10,11... | collective-permute-start | bytes 786440 | tf_op jit(solution)/shard_map/ppermute | solution.py:27
  10.1 26.0 %collective-permute-start.5 = (bf16[1024,128]{1,0:T(8,128)(2,1)}, bf16[1024,128]{1,0:T(8,128)(2,1)}, u32[]{:S(2)}, u32[]{:S(2)}) collective-permute-start(bf16[1024,128]{1,0:T(8,128)(2,1)} %convolution_convert_fusion.1), channel_id=1, source_target_pairs={{0,2},{1,3},{2,0},{3,1},{4,6},{5,7},{6,4},{7,5},{8,10},{9,11},{10,... | collective-permute-start | bytes 786440 | tf_op jit(solution)/shard_map/ppermute | solution.py:27
  11.0 54.2 %collective-permute-start.6 = (bf16[1024,384]{1,0:T(8,128)(2,1)S(1)}, bf16[1024,384]{1,0:T(8,128)(2,1)S(1)}, u32[]{:S(2)}, u32[]{:S(2)}) collective-permute-start(bf16[1024,384]{1,0:T(8,128)(2,1)S(1)} %convolution_convert_fusion), channel_id=1, source_target_pairs={{0,2},{1,3},{2,0},{3,1},{4,6},{5,7},{6,4},{7,5},{8,10},{9,11},{10,... | collective-permute-start | bytes 2359304 | tf_op jit(solution)/shard_map/ppermute | solution.py:27
  20.9 56.5 %collective-permute-start.7 = (f32[2048,128]{1,0:T(8,128)S(1)}, f32[2048,128]{1,0:T(8,128)S(1)}, u32[]{:S(2)}, u32[]{:S(2)}) collective-permute-start(f32[2048,128]{1,0:T(8,128)S(1)} %get-tuple-element.43), channel_id=1, source_target_pairs={{0,64},{1,5},{2,66},{3,7},{4,68},{5,9},{6,70},{7,11},{8,72},{9,13}... | collective-permute-start | bytes 3145736 | tf_op jit(solution)/shard_map/ppermute | solution.py:27
  36.1 41.3 %collective-permute-start.8 = (f32[2048,128]{1,0:T(8,128)S(1)}, f32[2048,128]{1,0:T(8,128)S(1)}, u32[]{:S(2)}, u32[]{:S(2)}) collective-permute-start(f32[2048,128]{1,0:T(8,128)S(1)} %get-tuple-element.44), channel_id=1, source_target_pairs={{0,128},{1,9},{2,130},{3,11},{4,132},{5,13},{6,134},{7,15},{8,136}... | collective-permute-start | bytes 3145736 | tf_op jit(solution)/shard_map/ppermute | solution.py:27
  39.1 38.3 %collective-permute-start.9 = (f32[2048,128]{1,0:T(8,128)S(1)}, f32[2048,128]{1,0:T(8,128)S(1)}, u32[]{:S(2)}, u32[]{:S(2)}) collective-permute-start(f32[2048,128]{1,0:T(8,128)S(1)} %get-tuple-element.45), channel_id=1, source_target_pairs={{0,192},{1,13},{2,194},{3,15},{4,196},{5,1},{6,198},{7,3},{8,200},... | collective-permute-start | bytes 3145736 | tf_op jit(solution)/shard_map/ppermute | solution.py:27
  45.0 23.3 %collective-permute-start.10 = (f32[640,128]{1,0:T(8,128)S(1)}, f32[640,128]{1,0:T(8,128)S(1)}, u32[]{:S(2)}, u32[]{:S(2)}) collective-permute-start(f32[640,128]{1,0:T(8,128)S(1)} %get-tuple-element.46), channel_id=1, source_target_pairs={{0,64},{1,5},{2,66},{3,7},{4,68},{5,9},{6,70},{7,11},{8,72},{9,13}... | collective-permute-start | bytes 983048 | tf_op jit(solution)/shard_map/ppermute | solution.py:27
  65.2 8.6 %collective-permute-start.11 = (f32[640,128]{1,0:T(8,128)S(1)}, f32[640,128]{1,0:T(8,128)S(1)}, u32[]{:S(2)}, u32[]{:S(2)}) collective-permute-start(f32[640,128]{1,0:T(8,128)S(1)} %get-tuple-element.47), channel_id=1, source_target_pairs={{0,128},{1,9},{2,130},{3,11},{4,132},{5,13},{6,134},{7,15},{8,136}... | collective-permute-start | bytes 983048 | tf_op jit(solution)/shard_map/ppermute | solution.py:27
  68.2 9.2 %collective-permute-start.12 = (f32[640,128]{1,0:T(8,128)S(1)}, f32[640,128]{1,0:T(8,128)S(1)}, u32[]{:S(2)}, u32[]{:S(2)}) collective-permute-start(f32[640,128]{1,0:T(8,128)S(1)} %get-tuple-element.48), channel_id=1, source_target_pairs={{0,192},{1,13},{2,194},{3,15},{4,196},{5,1},{6,198},{7,3},{8,200},... | collective-permute-start | bytes 983048 | tf_op jit(solution)/shard_map/ppermute | solution.py:27
  78.3 12.2 %collective-permute-start.13 = (f32[672,128]{1,0:T(8,128)S(1)}, f32[672,128]{1,0:T(8,128)S(1)}, u32[]{:S(2)}, u32[]{:S(2)}) collective-permute-start(f32[672,128]{1,0:T(8,128)S(1)} %get-tuple-element.50), channel_id=1, source_target_pairs={{0,4},{1,65},{2,6},{3,67},{4,8},{5,69},{6,10},{7,71},{8,12},{9,73}... | collective-permute-start | bytes 1032200 | tf_op jit(solution)/shard_map/ppermute | solution.py:27
  79.9 37.4 %collective-permute-start.19 = (f32[1536,128]{1,0:T(8,128)S(1)}, f32[1536,128]{1,0:T(8,128)S(1)}, u32[]{:S(2)}, u32[]{:S(2)}) collective-permute-start(f32[1536,128]{1,0:T(8,128)S(1)} %get-tuple-element.58), channel_id=1, source_target_pairs={{0,64},{1,5},{2,66},{3,7},{4,68},{5,9},{6,70},{7,11},{8,72},{9,13}... | collective-permute-start | bytes 2359304 | tf_op jit(solution)/shard_map/ppermute | solution.py:27
  81.3 36.0 %collective-permute-start.20 = (f32[1536,128]{1,0:T(8,128)S(1)}, f32[1536,128]{1,0:T(8,128)S(1)}, u32[]{:S(2)}, u32[]{:S(2)}) collective-permute-start(f32[1536,128]{1,0:T(8,128)S(1)} %get-tuple-element.59), channel_id=1, source_target_pairs={{0,128},{1,9},{2,130},{3,11},{4,132},{5,13},{6,134},{7,15},{8,136}... | collective-permute-start | bytes 2359304 | tf_op jit(solution)/shard_map/ppermute | solution.py:27
  84.0 33.3 %collective-permute-start.21 = (f32[1536,128]{1,0:T(8,128)S(1)}, f32[1536,128]{1,0:T(8,128)S(1)}, u32[]{:S(2)}, u32[]{:S(2)}) collective-permute-start(f32[1536,128]{1,0:T(8,128)S(1)} %get-tuple-element.60), channel_id=1, source_target_pairs={{0,192},{1,13},{2,194},{3,15},{4,196},{5,1},{6,198},{7,3},{8,200},... | collective-permute-start | bytes 2359304 | tf_op jit(solution)/shard_map/ppermute | solution.py:27
  84.6 14.6 %collective-permute-start.14 = (f32[672,128]{1,0:T(8,128)S(1)}, f32[672,128]{1,0:T(8,128)S(1)}, u32[]{:S(2)}, u32[]{:S(2)}) collective-permute-start(f32[672,128]{1,0:T(8,128)S(1)} %get-tuple-element.51), channel_id=1, source_target_pairs={{0,8},{1,129},{2,10},{3,131},{4,12},{5,133},{6,14},{7,135},{8,0},{... | collective-permute-start | bytes 1032200 | tf_op jit(solution)/shard_map/ppermute | solution.py:27
  90.5 13.0 %collective-permute-start.15 = (f32[672,128]{1,0:T(8,128)S(1)}, f32[672,128]{1,0:T(8,128)S(1)}, u32[]{:S(2)}, u32[]{:S(2)}) collective-permute-start(f32[672,128]{1,0:T(8,128)S(1)} %get-tuple-element.52), channel_id=1, source_target_pairs={{0,12},{1,193},{2,14},{3,195},{4,0},{5,197},{6,2},{7,199},{8,4},{9... | collective-permute-start | bytes 1032200 | tf_op jit(solution)/shard_map/ppermute | solution.py:27
  104.0 6.4 %collective-permute-start.16 = (f32[168,128]{1,0:T(8,128)S(1)}, f32[168,128]{1,0:T(8,128)S(1)}, u32[]{:S(2)}, u32[]{:S(2)}) collective-permute-start(f32[168,128]{1,0:T(8,128)S(1)} %get-tuple-element.54), channel_id=1, source_target_pairs={{0,16},{1,17},{2,18},{3,19},{4,20},{5,21},{6,22},{7,23},{8,24},{9,... | collective-permute-start | bytes 258056 | tf_op jit(solution)/shard_map/ppermute | solution.py:27
  104.1 10.6 %collective-permute-start.17 = (f32[168,128]{1,0:T(8,128)S(1)}, f32[168,128]{1,0:T(8,128)S(1)}, u32[]{:S(2)}, u32[]{:S(2)}) collective-permute-start(f32[168,128]{1,0:T(8,128)S(1)} %get-tuple-element.55), channel_id=1, source_target_pairs={{0,32},{1,33},{2,34},{3,35},{4,36},{5,37},{6,38},{7,39},{8,40},{9,... | collective-permute-start | bytes 258056 | tf_op jit(solution)/shard_map/ppermute | solution.py:27
  110.5 6.8 %collective-permute-start.18 = (f32[168,128]{1,0:T(8,128)S(1)}, f32[168,128]{1,0:T(8,128)S(1)}, u32[]{:S(2)}, u32[]{:S(2)}) collective-permute-start(f32[168,128]{1,0:T(8,128)S(1)} %get-tuple-element.56), channel_id=1, source_target_pairs={{0,48},{1,49},{2,50},{3,51},{4,52},{5,53},{6,54},{7,55},{8,56},{9,... | collective-permute-start | bytes 258056 | tf_op jit(solution)/shard_map/ppermute | solution.py:27
  118.1 9.2 %collective-permute-start.22 = (f32[392,128]{1,0:T(8,128)S(1)}, f32[392,128]{1,0:T(8,128)S(1)}, u32[]{:S(2)}, u32[]{:S(2)}) collective-permute-start(f32[392,128]{1,0:T(8,128)S(1)} %get-tuple-element.62), channel_id=1, source_target_pairs={{0,4},{1,65},{2,6},{3,67},{4,8},{5,69},{6,10},{7,71},{8,12},{9,73}... | collective-permute-start | bytes 602120 | tf_op jit(solution)/shard_map/ppermute | solution.py:27
  118.3 9.0 %collective-permute-start.23 = (f32[392,128]{1,0:T(8,128)S(1)}, f32[392,128]{1,0:T(8,128)S(1)}, u32[]{:S(2)}, u32[]{:S(2)}) collective-permute-start(f32[392,128]{1,0:T(8,128)S(1)} %get-tuple-element.63), channel_id=1, source_target_pairs={{0,8},{1,129},{2,10},{3,131},{4,12},{5,133},{6,14},{7,135},{8,0},{... | collective-permute-start | bytes 602120 | tf_op jit(solution)/shard_map/ppermute | solution.py:27
  120.7 7.4 %collective-permute-start.24 = (f32[392,128]{1,0:T(8,128)S(1)}, f32[392,128]{1,0:T(8,128)S(1)}, u32[]{:S(2)}, u32[]{:S(2)}) collective-permute-start(f32[392,128]{1,0:T(8,128)S(1)} %get-tuple-element.64), channel_id=1, source_target_pairs={{0,12},{1,193},{2,14},{3,195},{4,0},{5,197},{6,2},{7,199},{8,4},{9... | collective-permute-start | bytes 602120 | tf_op jit(solution)/shard_map/ppermute | solution.py:27
  128.7 5.0 %collective-permute-start.25 = (f32[128,128]{1,0:T(8,128)S(1)}, f32[128,128]{1,0:T(8,128)S(1)}, u32[]{:S(2)}, u32[]{:S(2)}) collective-permute-start(f32[128,128]{1,0:T(8,128)S(1)} %get-tuple-element.66), channel_id=1, source_target_pairs={{0,16},{1,17},{2,18},{3,19},{4,20},{5,21},{6,22},{7,23},{8,24},{9,... | collective-permute-start | bytes 196616 | tf_op jit(solution)/shard_map/ppermute | solution.py:27
  129.0 7.0 %collective-permute-start.26 = (f32[128,128]{1,0:T(8,128)S(1)}, f32[128,128]{1,0:T(8,128)S(1)}, u32[]{:S(2)}, u32[]{:S(2)}) collective-permute-start(f32[128,128]{1,0:T(8,128)S(1)} %get-tuple-element.67), channel_id=1, source_target_pairs={{0,32},{1,33},{2,34},{3,35},{4,36},{5,37},{6,38},{7,39},{8,40},{9,... | collective-permute-start | bytes 196616 | tf_op jit(solution)/shard_map/ppermute | solution.py:27
  133.0 4.3 %collective-permute-start.27 = (f32[128,128]{1,0:T(8,128)S(1)}, f32[128,128]{1,0:T(8,128)S(1)}, u32[]{:S(2)}, u32[]{:S(2)}) collective-permute-start(f32[128,128]{1,0:T(8,128)S(1)} %get-tuple-element.68), channel_id=1, source_target_pairs={{0,48},{1,49},{2,50},{3,51},{4,52},{5,53},{6,54},{7,55},{8,56},{9,... | collective-permute-start | bytes 196616 | tf_op jit(solution)/shard_map/ppermute | solution.py:27
  137.3 9.8 %collective-permute-start.28 = (f32[128,128]{1,0:T(8,128)S(1)}, f32[128,128]{1,0:T(8,128)S(1)}, u32[]{:S(2)}, u32[]{:S(2)}) collective-permute-start(f32[128,128]{1,0:T(8,128)S(1)} %pad_maximum_fusion.a), channel_id=1, source_target_pairs={{0,64},{1,5},{2,66},{3,7},{4,68},{5,9},{6,70},{7,11},{8,72},{9,13}... | collective-permute-start | bytes 196616 | tf_op jit(solution)/shard_map/ppermute | solution.py:27
  139.2 7.9 %collective-permute-start.29 = (f32[128,128]{1,0:T(8,128)S(1)}, f32[128,128]{1,0:T(8,128)S(1)}, u32[]{:S(2)}, u32[]{:S(2)}) collective-permute-start(f32[128,128]{1,0:T(8,128)S(1)} %pad_maximum_fusion.a), channel_id=1, source_target_pairs={{0,128},{1,9},{2,130},{3,11},{4,132},{5,13},{6,134},{7,15},{8,136}... | collective-permute-start | bytes 196616 | tf_op jit(solution)/shard_map/ppermute | solution.py:27
  141.1 6.1 %collective-permute-start.30 = (f32[128,128]{1,0:T(8,128)S(1)}, f32[128,128]{1,0:T(8,128)S(1)}, u32[]{:S(2)}, u32[]{:S(2)}) collective-permute-start(f32[128,128]{1,0:T(8,128)S(1)} %pad_maximum_fusion.a), channel_id=1, source_target_pairs={{0,192},{1,13},{2,194},{3,15},{4,196},{5,1},{6,198},{7,3},{8,200},... | collective-permute-start | bytes 196616 | tf_op jit(solution)/shard_map/ppermute | solution.py:27
  142.5 6.0 %collective-permute-start.31 = (f32[128,128]{1,0:T(8,128)S(1)}, f32[128,128]{1,0:T(8,128)S(1)}, u32[]{:S(2)}, u32[]{:S(2)}) collective-permute-start(f32[128,128]{1,0:T(8,128)S(1)} %get-tuple-element.71), channel_id=1, source_target_pairs={{0,2},{1,3},{2,130},{3,131},{4,6},{5,7},{6,134},{7,135},{8,10},{9,... | collective-permute-start | bytes 196616 | tf_op jit(solution)/shard_map/ppermute | solution.py:27
  146.3 2.3 %collective-permute-start.32 = (f32[128,128]{1,0:T(8,128)S(1)}, f32[128,128]{1,0:T(8,128)S(1)}, u32[]{:S(2)}, u32[]{:S(2)}) collective-permute-start(f32[128,128]{1,0:T(8,128)S(1)} %get-tuple-element.73.cross), channel_id=1, source_target_pairs={{3,66},{7,70},{11,74},{15,78},{19,82},{23,86},{27,90},{31,94},{35,... | collective-permute-start | bytes 196616 | tf_op jit(solution)/shard_map/ppermute | solution.py:27
  (4 other events, 8.7 us)
where the time goes:
time: 151 us; the launch traced here: 150 us
  waiting for transfers between devices  66.5 us (44%)
  starting transfers between devices  63.2 us (42%)
  Pallas kernels  15.3 us (10%)
  matrix products  3.28 us (2%)
    ppermute x33, waiting for transfers between devices, move(): return lax.ppermute(values, AXES, pairs)  66.5 us
    ppermute x33, starting transfers between devices, move(): return lax.ppermute(values, AXES, pairs)  63.2 us
    pallas_call x3, Pallas kernels, blocks_call(): pl.pallas_call(kernel, out_shape=outs, in_specs=[SMEM] + [VMEM] * len(ope...  9.79 us
    pallas_call x6, Pallas kernels, sums_call(): pl.pallas_call(kernel, out_shape=outs, in_specs=[SMEM] * len(head) + [VME...  5.49 us
    dot_general x2, matrix products, shards(): jnp.dot(chosen, pick.astype(jnp.bfloat16), preferred_element_type=F32)  3.28 us
  transfers between devices with their start and end apart: 33, of which 16 were waited for; matrix products, arithmetic and copies ran while one was open for 3% of the time, Pallas kernels for 8%

commit v1 on v0

--- a/solution.py
+++ b/solution.py
@@ -143,11 +143,9 @@
     emit(room, outs, sems)
 
 
-def middle_kernel(sizes, gathered, scalars, *refs):
+def middle_kernel(sizes, scalars, *refs):
     x, y, zh, core = scalars[0], scalars[1], scalars[3], scalars[4]
     ins, outs = refs[:-4], refs[-4:]
-    if gathered:
-        piece, ins = ins[-1], ins[:-1]
     each = len(ins) // len(sizes)
     is0 = core == 0
     whole = sum(sizes)
@@ -165,31 +163,29 @@
                     total += r[at]
                 out[start : start + size] = total
                 start += size
-        if gathered:
-            out[4 * whole : 4 * whole + 8] = piece[...]
-
-
-def last_kernel(size, gathered, scalars, a, b, c, d, *outs):
+
+
+def last_kernel(size, scalars, a, b, c, d, *rest):
     zl = scalars[2]
+    more, outs = rest[:-4], rest[-4:]
     for j, out in enumerate(outs):
         at = rows_at(lax.rem(zl + j, 4), size, 0, size)
         out[:size] = (a[at] + b[at]) + (c[at] + d[at])
-        if gathered:
-            for n, r in enumerate((a, b, c, d)):
-                out[size + 8 * n : size + 8 * (n + 1)] = r[4 * size : 4 * size + 8]
+        for piece in more:
+            out[size:] = piece[...]
 
 
 def latent_kernel(scale, scalars, a, b, c, d, out):
     x, y, zl, core = scalars[0], scalars[1], scalars[2], scalars[4]
     is0 = core == 0
-    for j1, ref in enumerate((a, b, c, d)):
-        for jz in range(4):
-            for j2 in range(4):
+    for j2, ref in enumerate((a, b, c, d)):
+        for j1 in range(4):
+            for jz in range(4):
                 xb = lax.rem(x + 4 - jnp.where(is0, j1, j2), 4)
                 yb = lax.rem(y + 4 - jnp.where(is0, j2, j1), 4)
                 zb = lax.rem(zl + 4 - jz, 4)
                 to = rows_at(16 * xb + 4 * zb + yb, 8, 0, 8)
-                at = 32 * jz + 8 * j2
+                at = 32 * j1 + 8 * jz
                 out[to, :] = ref[at : at + 8, :] * scale
 
 
@@ -300,15 +296,13 @@
     near = jnp.where(low, grad_key, grad_value)
     near_other = jnp.where(low, key_other, value_other)
 
-    def middle(sizes, *parts, gathered=False, gate):
-        shape = (4 * sum(sizes) + (8 if gathered else 0), 128)
-        kernel = functools.partial(middle_kernel, sizes, gathered)
-        return sums_call(kernel, [shape] * 4, after(scalars, gate), *parts)
-
-    def last(size, *parts, gathered=False, gate=()):
-        shape = (size + (32 if gathered else 0), 128)
-        kernel = functools.partial(last_kernel, size, gathered)
-        return sums_call(kernel, [shape] * 4, after(scalars, gate), *parts)
+    def middle(sizes, *parts, gate):
+        kernel = functools.partial(middle_kernel, sizes)
+        return sums_call(kernel, [(4 * sum(sizes), 128)] * 4, after(scalars, gate), *parts)
+
+    def last(size, *parts):
+        rows = size + sum(p.shape[0] for p in parts[4:])
+        return sums_call(functools.partial(last_kernel, size), [(rows, 128)] * 4, scalars, *parts)
 
     own = blocks_call(
         own_kernel, 16 * 128, scalars, grad_key, key_other, grad_value, value_other
@@ -331,16 +325,17 @@
     c0 = exchange(last(168, *c0), along_z)
     c0 = (c0[0] + c0[1]) + (c0[2] + c0[3])
     own = c0[:128]
-    c = middle((96,), *c1, c0[160:], gathered=True, gate=c0)
+    c = middle((96,), *c1, gate=gate)
     c = exchange(c, second)
-    c = exchange(last(96, *c, gathered=True), along_z)
+    c = exchange(last(96, *c, c0[160:]), along_z)
     pieces = jnp.concatenate([part[96:] for part in c], axis=0)
     ends = (c[0][:96] + c[1][:96]) + (c[2][:96] + c[3][:96])
     crossed = jnp.concatenate([c0[128:160], ends], axis=0)
+    pieces = jnp.concatenate(exchange([pieces] * 4, first), axis=0)
     moved = move(jnp.where(x // 2 == zh, crossed, own), homeward)
     turned = move(crossed, sideways)
     (latent_sum,) = sums_call(
-        functools.partial(latent_kernel, scale), [(512, 128)], scalars, *exchange([pieces] * 4, first)
+        functools.partial(latent_kernel, scale), [(512, 128)], scalars, *exchange([pieces] * 4, second)
     )
     key_sum, value_sum = sums_call(
         functools.partial(finish_kernel, scale), [(32, width)] * 2, scalars, own, crossed, moved, turned, order

time: 151 us -> 152 us (level)
  waiting for transfers between devices: 66.5 us -> 61.4 us
  starting transfers between devices: 63.2 us -> 68.1 us
    ppermute x33 -> x36, waiting for transfers between devices: 66.5 us -> 61.4 us  [move(): return lax.ppermute(values, AXES, pairs)]
    ppermute x33 -> x36, starting transfers between devices: 63.2 us -> 68.1 us  [move(): return lax.ppermute(values, AXES, pairs)]
  transfers between devices with their start and end apart: 33 -> 36, of which waited for: 16 -> 14; matrix products, arithmetic and copies ran while one was open for 3% -> 3% of each run, Pallas kernels for 8% -> 9%
where the time goes in v1:
time: 152 us; the launch traced here: 151 us
  starting transfers between devices  68.1 us (45%)
  waiting for transfers between devices  61.4 us (40%)
  Pallas kernels  16.2 us (11%)
  matrix products  3.28 us (2%)
    ppermute x36, starting transfers between devices, move(): return lax.ppermute(values, AXES, pairs)  68.1 us
    ppermute x36, waiting for transfers between devices, move(): return lax.ppermute(values, AXES, pairs)  61.4 us
    pallas_call x3, Pallas kernels, blocks_call(): pl.pallas_call(kernel, out_shape=outs, in_specs=[SMEM] + [VMEM] * len(ope...  10.9 us
    pallas_call x6, Pallas kernels, sums_call(): pl.pallas_call(kernel, out_shape=outs, in_specs=[SMEM] * len(head) + [VME...  5.37 us
    dot_general x2, matrix products, shards(): jnp.dot(chosen, pick.astype(jnp.bfloat16), preferred_element_type=F32)  3.28 us
  transfers between devices with their start and end apart: 36, of which 14 were waited for; matrix products, arithmetic and copies ran while one was open for 3% of the time, Pallas kernels for 9%

profile of v1, /device:TPU:32, one launch (start us, length us, event | category | flops | bytes accessed | tf_op | source)
XLA Modules:
  0.0 151.5 jit_solution(16357410489618351161)
XLA Ops:
  1.2 6.3 %collective-permute-start.3 = (bf16[1024,128]{1,0:T(8,128)(2,1)}, bf16[1024,128]{1,0:T(8,128)(2,1)S(1)}, u32[]{:S(2)}, u32[]{:S(2)}) collective-permute-start(bf16[1024,128]{1,0:T(8,128)(2,1)} %rest_0_.1), channel_id=1, source_target_pairs={{0,2},{1,3},{2,0},{3,1},{4,6},{5,7},{6,4},{7,5},{8,10},{9,11},{10,... | collective-permute-start | bytes 786440 | tf_op jit(solution)/shard_map/ppermute | solution.py:27
  7.6 2.5 %convolution_convert_fusion.1 = bf16[1024,128]{1,0:T(8,128)(2,1)} fusion(bf16[1024,512]{1,0:T(8,128)(2,1)} %vm.1, bf16[1024,512]{1,0:T(8,128)(2,1)} %km.1, pred[]{:T(512)S(6)} %eq.49, s32[128]{0:T(128)S(1)} %slice.39), kind=kOutput, calls=%fused_computation.1 | convolution fusion | flops 134938624 | bytes 2359809 | tf_op jit(solution)/shard_map/dot_general | solution.py:286
  11.0 5.9 %collective-permute-start.6 = (bf16[1024,384]{1,0:T(8,128)(2,1)S(1)}, bf16[1024,384]{1,0:T(8,128)(2,1)S(1)}, u32[]{:S(2)}, u32[]{:S(2)}) collective-permute-start(bf16[1024,384]{1,0:T(8,128)(2,1)S(1)} %convolution_convert_fusion), channel_id=1, source_target_pairs={{0,2},{1,3},{2,0},{3,1},{4,6},{5,7},{6,4},{7,5},{8,10},{9,11},{10,... | collective-permute-start | bytes 2359304 | tf_op jit(solution)/shard_map/ppermute | solution.py:27
  17.0 3.9 %shard_map.58 = (f32[2048,128]{1,0:T(8,128)S(1)}, f32[2048,128]{1,0:T(8,128)S(1)}, f32[2048,128]{1,0:T(8,128)S(1)}, f32[2048,128]{1,0:T(8,128)S(1)}) custom-call(s32[5]{0:T(128)S(1)} %stack.23.scalars, bf16[1024,512]{1,0:T(8,128)(2,1)S(1)} %copy-done, bf16[1024,512]{1,0:T(8,128)(2,1)S(1)} %collective-permute-done.ko, bf16[1024,512]{1,0:T(8,128)(2,1)S(1)} %copy-done.1, ...), custom_call_target="tpu_custom_call" | custom-call | tf_op jit(solution)/shard_map/pallas_call | solution.py:240
  22.5 13.6 %collective-permute-done.5.rest_4_ = bf16[1024,128]{1,0:T(8,128)(2,1)} collective-permute-done((bf16[1024,128]{1,0:T(8,128)(2,1)}, bf16[1024,128]{1,0:T(8,128)(2,1)}, u32[]{:S(2)}, u32[]{:S(2)}) %collective-permute-start.5) | collective-permute-done | bytes 262176 | tf_op jit(solution)/shard_map/ppermute | solution.py:27
  36.1 3.0 %collective-permute-start.14 = (f32[2048,128]{1,0:T(8,128)S(1)}, f32[2048,128]{1,0:T(8,128)S(1)}, u32[]{:S(2)}, u32[]{:S(2)}) collective-permute-start(f32[2048,128]{1,0:T(8,128)S(1)} %get-tuple-element.50), channel_id=1, source_target_pairs={{0,128},{1,9},{2,130},{3,11},{4,132},{5,13},{6,134},{7,15},{8,136}... | collective-permute-start | bytes 3145736 | tf_op jit(solution)/shard_map/ppermute | solution.py:27
  42.0 2.9 %shard_map.59 = (f32[640,128]{1,0:T(8,128)S(1)}, f32[640,128]{1,0:T(8,128)S(1)}, f32[640,128]{1,0:T(8,128)S(1)}, f32[640,128]{1,0:T(8,128)S(1)}) custom-call(s32[5]{0:T(128)S(1)} %stack.23.scalars, bf16[1024,512]{1,0:T(8,128)(2,1)S(1)} %broadcast_select_fusion.2.nm, bf16[1024,512]{1,0:T(8,128)(2,1)S(1)} %broadcast_select_fusion.1.no, ...), custom_call_target="tpu_custom_call" | custom-call | tf_op jit(solution)/shard_map/pallas_call | solution.py:240
  45.9 19.3 %collective-permute-done.6.rest_0_ = bf16[1024,384]{1,0:T(8,128)(2,1)S(1)} collective-permute-done((bf16[1024,384]{1,0:T(8,128)(2,1)S(1)}, bf16[1024,384]{1,0:T(8,128)(2,1)S(1)}, u32[]{:S(2)}, u32[]{:S(2)}) %collective-permute-start.6) | collective-permute-done | bytes 786464 | tf_op jit(solution)/shard_map/ppermute | solution.py:27
  65.2 3.0 %collective-permute-start.17 = (f32[640,128]{1,0:T(8,128)S(1)}, f32[640,128]{1,0:T(8,128)S(1)}, u32[]{:S(2)}, u32[]{:S(2)}) collective-permute-start(f32[640,128]{1,0:T(8,128)S(1)} %get-tuple-element.53), channel_id=1, source_target_pairs={{0,128},{1,9},{2,130},{3,11},{4,132},{5,13},{6,134},{7,15},{8,136}... | collective-permute-start | bytes 983048 | tf_op jit(solution)/shard_map/ppermute | solution.py:27
  69.4 4.0 %shard_map.60 = (f32[1536,128]{1,0:T(8,128)S(1)}, f32[1536,128]{1,0:T(8,128)S(1)}, f32[1536,128]{1,0:T(8,128)}, f32[1536,128]{1,0:T(8,128)}) custom-call(s32[5]{0:T(128)S(1)} %stack.23.scalars, bf16[1024,512]{1,0:T(8,128)(2,1)S(1)} %broadcast_select_fusion.2.nm, bf16[1024,512]{1,0:T(8,128)(2,1)S(1)} %broadcast_select_fusion.1.no, ...), custom_call_target="tpu_custom_call" | custom-call | tf_op jit(solution)/shard_map/pallas_call | solution.py:240
  73.8 1.6 %collective-permute-start.7 = (f32[1536,128]{1,0:T(8,128)S(1)}, f32[1536,128]{1,0:T(8,128)S(1)}, u32[]{:S(2)}, u32[]{:S(2)}) collective-permute-start(f32[1536,128]{1,0:T(8,128)S(1)} %get-tuple-element.41), channel_id=1, source_target_pairs={{0,64},{1,5},{2,66},{3,7},{4,68},{5,9},{6,70},{7,11},{8,72},{9,13}... | collective-permute-start | bytes 2359304 | tf_op jit(solution)/shard_map/ppermute | solution.py:27
  75.4 2.0 %collective-permute-done.18.refs_7_ = f32[640,128]{1,0:T(8,128)S(1)} collective-permute-done((f32[640,128]{1,0:T(8,128)S(1)}, f32[640,128]{1,0:T(8,128)S(1)}, u32[]{:S(2)}, u32[]{:S(2)}) %collective-permute-start.18) | collective-permute-done | bytes 327712 | tf_op jit(solution)/shard_map/ppermute | solution.py:27
  77.4 2.0 %collective-permute-start.8 = (f32[1536,128]{1,0:T(8,128)}, f32[1536,128]{1,0:T(8,128)S(1)}, u32[]{:S(2)}, u32[]{:S(2)}) collective-permute-start(f32[1536,128]{1,0:T(8,128)} %get-tuple-element.42), channel_id=1, source_target_pairs={{0,128},{1,9},{2,130},{3,11},{4,132},{5,13},{6,134},{7,15},{8,136}... | collective-permute-start | bytes 2359304 | tf_op jit(solution)/shard_map/ppermute | solution.py:27
  79.4 2.0 %collective-permute-start.9 = (f32[1536,128]{1,0:T(8,128)}, f32[1536,128]{1,0:T(8,128)S(1)}, u32[]{:S(2)}, u32[]{:S(2)}) collective-permute-start(f32[1536,128]{1,0:T(8,128)} %get-tuple-element.43), channel_id=1, source_target_pairs={{0,192},{1,13},{2,194},{3,15},{4,196},{5,1},{6,198},{7,3},{8,200},... | collective-permute-start | bytes 2359304 | tf_op jit(solution)/shard_map/ppermute | solution.py:27
  82.3 1.7 %collective-permute-start.19 = (f32[672,128]{1,0:T(8,128)S(1)}, f32[672,128]{1,0:T(8,128)S(1)}, u32[]{:S(2)}, u32[]{:S(2)}) collective-permute-start(f32[672,128]{1,0:T(8,128)S(1)} %get-tuple-element.56), channel_id=1, source_target_pairs={{0,4},{1,65},{2,6},{3,67},{4,8},{5,69},{6,10},{7,71},{8,12},{9,73}... | collective-permute-start | bytes 1032200 | tf_op jit(solution)/shard_map/ppermute | solution.py:27
  83.9 2.9 %collective-permute-start.20 = (f32[672,128]{1,0:T(8,128)S(1)}, f32[672,128]{1,0:T(8,128)S(1)}, u32[]{:S(2)}, u32[]{:S(2)}) collective-permute-start(f32[672,128]{1,0:T(8,128)S(1)} %get-tuple-element.57), channel_id=1, source_target_pairs={{0,8},{1,129},{2,10},{3,131},{4,12},{5,133},{6,14},{7,135},{8,0},{... | collective-permute-start | bytes 1032200 | tf_op jit(solution)/shard_map/ppermute | solution.py:27
  86.8 9.0 %collective-permute-done.19.b = f32[672,128]{1,0:T(8,128)S(1)} collective-permute-done((f32[672,128]{1,0:T(8,128)S(1)}, f32[672,128]{1,0:T(8,128)S(1)}, u32[]{:S(2)}, u32[]{:S(2)}) %collective-permute-start.19) | collective-permute-done | bytes 344096 | tf_op jit(solution)/shard_map/ppermute | solution.py:27
  96.4 5.3 %collective-permute-done.20.c = f32[672,128]{1,0:T(8,128)S(1)} collective-permute-done((f32[672,128]{1,0:T(8,128)S(1)}, f32[672,128]{1,0:T(8,128)S(1)}, u32[]{:S(2)}, u32[]{:S(2)}) %collective-permute-start.20) | collective-permute-done | bytes 344096 | tf_op jit(solution)/shard_map/ppermute | solution.py:27
  101.7 2.8 %collective-permute-done.21.d = f32[672,128]{1,0:T(8,128)S(1)} collective-permute-done((f32[672,128]{1,0:T(8,128)S(1)}, f32[672,128]{1,0:T(8,128)S(1)}, u32[]{:S(2)}, u32[]{:S(2)}) %collective-permute-start.21) | collective-permute-done | bytes 344096 | tf_op jit(solution)/shard_map/ppermute | solution.py:27
  105.2 5.6 %collective-permute-start.23 = (f32[168,128]{1,0:T(8,128)S(1)}, f32[168,128]{1,0:T(8,128)}, u32[]{:S(2)}, u32[]{:S(2)}) collective-permute-start(f32[168,128]{1,0:T(8,128)S(1)} %get-tuple-element.61), channel_id=1, source_target_pairs={{0,32},{1,33},{2,34},{3,35},{4,36},{5,37},{6,38},{7,39},{8,40},{9,... | collective-permute-start | bytes 258056 | tf_op jit(solution)/shard_map/ppermute | solution.py:27
  111.5 3.1 %collective-permute-start.10 = (f32[384,128]{1,0:T(8,128)S(1)}, f32[384,128]{1,0:T(8,128)S(1)}, u32[]{:S(2)}, u32[]{:S(2)}) collective-permute-start(f32[384,128]{1,0:T(8,128)S(1)} %get-tuple-element.45), channel_id=1, source_target_pairs={{0,4},{1,65},{2,6},{3,67},{4,8},{5,69},{6,10},{7,71},{8,12},{9,73}... | collective-permute-start | bytes 589832 | tf_op jit(solution)/shard_map/ppermute | solution.py:27
  114.6 2.2 %collective-permute-start.11 = (f32[384,128]{1,0:T(8,128)S(1)}, f32[384,128]{1,0:T(8,128)S(1)}, u32[]{:S(2)}, u32[]{:S(2)}) collective-permute-start(f32[384,128]{1,0:T(8,128)S(1)} %get-tuple-element.46), channel_id=1, source_target_pairs={{0,8},{1,129},{2,10},{3,131},{4,12},{5,133},{6,14},{7,135},{8,0},{... | collective-permute-start | bytes 589832 | tf_op jit(solution)/shard_map/ppermute | solution.py:27
  116.8 2.5 %collective-permute-start.12 = (f32[384,128]{1,0:T(8,128)S(1)}, f32[384,128]{1,0:T(8,128)S(1)}, u32[]{:S(2)}, u32[]{:S(2)}) collective-permute-start(f32[384,128]{1,0:T(8,128)S(1)} %get-tuple-element.47), channel_id=1, source_target_pairs={{0,12},{1,193},{2,14},{3,195},{4,0},{5,197},{6,2},{7,199},{8,4},{9... | collective-permute-start | bytes 589832 | tf_op jit(solution)/shard_map/ppermute | solution.py:27
  120.3 2.1 %collective-permute-done.11.c = f32[384,128]{1,0:T(8,128)S(1)} collective-permute-done((f32[384,128]{1,0:T(8,128)S(1)}, f32[384,128]{1,0:T(8,128)S(1)}, u32[]{:S(2)}, u32[]{:S(2)}) %collective-permute-start.11) | collective-permute-done | bytes 196640 | tf_op jit(solution)/shard_map/ppermute | solution.py:27
  123.1 2.3 %collective-permute-start.25 = (f32[104,128]{1,0:T(8,128)S(1)}, f32[104,128]{1,0:T(8,128)S(1)}, u32[]{:S(2)}, u32[]{:S(2)}) collective-permute-start(f32[104,128]{1,0:T(8,128)S(1)} %get-tuple-element.64), channel_id=1, source_target_pairs={{0,16},{1,17},{2,18},{3,19},{4,20},{5,21},{6,22},{7,23},{8,24},{9,... | collective-permute-start | bytes 159752 | tf_op jit(solution)/shard_map/ppermute | solution.py:27
  125.4 1.8 %collective-permute-start.26 = (f32[104,128]{1,0:T(8,128)S(1)}, f32[104,128]{1,0:T(8,128)S(1)}, u32[]{:S(2)}, u32[]{:S(2)}) collective-permute-start(f32[104,128]{1,0:T(8,128)S(1)} %get-tuple-element.65), channel_id=1, source_target_pairs={{0,32},{1,33},{2,34},{3,35},{4,36},{5,37},{6,38},{7,39},{8,40},{9,... | collective-permute-start | bytes 159752 | tf_op jit(solution)/shard_map/ppermute | solution.py:27
  127.5 2.9 %collective-permute-done.26 = f32[104,128]{1,0:T(8,128)S(1)} collective-permute-done((f32[104,128]{1,0:T(8,128)S(1)}, f32[104,128]{1,0:T(8,128)S(1)}, u32[]{:S(2)}, u32[]{:S(2)}) %collective-permute-start.26) | collective-permute-done | bytes 53280 | tf_op jit(solution)/shard_map/ppermute | solution.py:27
  132.8 1.6 %collective-permute-start.29 = (f32[32,128]{1,0:T(8,128)S(1)}, f32[32,128]{1,0:T(8,128)S(1)}, u32[]{:S(2)}, u32[]{:S(2)}) collective-permute-start(f32[32,128]{1,0:T(8,128)S(1)} %pad_maximum_fusion.1), channel_id=1, source_target_pairs={{0,128},{1,9},{2,130},{3,11},{4,132},{5,13},{6,134},{7,15},{8,136}... | collective-permute-start | bytes 49160 | tf_op jit(solution)/shard_map/ppermute | solution.py:27
  134.5 2.5 %collective-permute-start.30 = (f32[32,128]{1,0:T(8,128)S(1)}, f32[32,128]{1,0:T(8,128)S(1)}, u32[]{:S(2)}, u32[]{:S(2)}) collective-permute-start(f32[32,128]{1,0:T(8,128)S(1)} %pad_maximum_fusion.1), channel_id=1, source_target_pairs={{0,192},{1,13},{2,194},{3,15},{4,196},{5,1},{6,198},{7,3},{8,200},... | collective-permute-start | bytes 49160 | tf_op jit(solution)/shard_map/ppermute | solution.py:27
  137.0 2.8 %collective-permute-start.34 = (f32[128,128]{1,0:T(8,128)S(1)}, f32[128,128]{1,0:T(8,128)S(1)}, u32[]{:S(2)}, u32[]{:S(2)}) collective-permute-start(f32[128,128]{1,0:T(8,128)S(1)} %get-tuple-element.69), channel_id=1, source_target_pairs={{0,2},{1,3},{2,130},{3,131},{4,6},{5,7},{6,134},{7,135},{8,10},{9,... | collective-permute-start | bytes 196616 | tf_op jit(solution)/shard_map/ppermute | solution.py:27
  140.6 2.0 %collective-permute-start.31 = (f32[128,128]{1,0:T(8,128)S(1)}, f32[128,128]{1,0:T(8,128)S(1)}, u32[]{:S(2)}, u32[]{:S(2)}) collective-permute-start(f32[128,128]{1,0:T(8,128)S(1)} %constant_dynamic-update-slice_fusion.a), channel_id=1, source_target_pairs={{0,4},{1,65},{2,6},{3,67},{4,8},{5,69},{6,10},{7,71},{8,12},{9,73}... | collective-permute-start | bytes 196616 | tf_op jit(solution)/shard_map/ppermute | solution.py:27
  142.6 3.2 %collective-permute-start.32 = (f32[128,128]{1,0:T(8,128)S(1)}, f32[128,128]{1,0:T(8,128)S(1)}, u32[]{:S(2)}, u32[]{:S(2)}) collective-permute-start(f32[128,128]{1,0:T(8,128)S(1)} %constant_dynamic-update-slice_fusion.a), channel_id=1, source_target_pairs={{0,8},{1,129},{2,10},{3,131},{4,12},{5,133},{6,14},{7,135},{8,0},{... | collective-permute-start | bytes 196616 | tf_op jit(solution)/shard_map/ppermute | solution.py:27
  (77 shorter events, 22.1 us)
Async XLA Ops:
  0.6 10.4 %collective-permute-start = (bf16[1024,512]{1,0:T(8,128)(2,1)}, bf16[1024,512]{1,0:T(8,128)(2,1)S(1)}, u32[]{:S(2)}, u32[]{:S(2)}) collective-permute-start(bf16[1024,512]{1,0:T(8,128)(2,1)} %km.1), channel_id=1, source_target_pairs={{0,1},{1,0},{2,3},{3,2},{4,5},{5,4},{6,7},{7,6},{8,9},{9,8},{10,11... | collective-permute-start | bytes 3145736 | tf_op jit(solution)/shard_map/ppermute | solution.py:27
  0.7 16.3 %collective-permute-start.1 = (bf16[1024,512]{1,0:T(8,128)(2,1)}, bf16[1024,512]{1,0:T(8,128)(2,1)}, u32[]{:S(2)}, u32[]{:S(2)}) collective-permute-start(bf16[1024,512]{1,0:T(8,128)(2,1)} %vm.1), channel_id=1, source_target_pairs={{0,1},{1,0},{2,3},{3,2},{4,5},{5,4},{6,7},{7,6},{8,9},{9,8},{10,11... | collective-permute-start | bytes 3145736 | tf_op jit(solution)/shard_map/ppermute | solution.py:27
  1.2 37.9 %collective-permute-start.3 = (bf16[1024,128]{1,0:T(8,128)(2,1)}, bf16[1024,128]{1,0:T(8,128)(2,1)S(1)}, u32[]{:S(2)}, u32[]{:S(2)}) collective-permute-start(bf16[1024,128]{1,0:T(8,128)(2,1)} %rest_0_.1), channel_id=1, source_target_pairs={{0,2},{1,3},{2,0},{3,1},{4,6},{5,7},{6,4},{7,5},{8,10},{9,11},{10,... | collective-permute-start | bytes 786440 | tf_op jit(solution)/shard_map/ppermute | solution.py:27
  7.5 32.9 %collective-permute-start.2 = (bf16[1024,128]{1,0:T(8,128)(2,1)}, bf16[1024,128]{1,0:T(8,128)(2,1)}, u32[]{:S(2)}, u32[]{:S(2)}) collective-permute-start(bf16[1024,128]{1,0:T(8,128)(2,1)} %rest_0_.1), channel_id=1, source_target_pairs={{0,1},{1,0},{2,3},{3,2},{4,5},{5,4},{6,7},{7,6},{8,9},{9,8},{10,11... | collective-permute-start | bytes 786440 | tf_op jit(solution)/shard_map/ppermute | solution.py:27
  10.1 26.0 %collective-permute-start.5 = (bf16[1024,128]{1,0:T(8,128)(2,1)}, bf16[1024,128]{1,0:T(8,128)(2,1)}, u32[]{:S(2)}, u32[]{:S(2)}) collective-permute-start(bf16[1024,128]{1,0:T(8,128)(2,1)} %convolution_convert_fusion.1), channel_id=1, source_target_pairs={{0,2},{1,3},{2,0},{3,1},{4,6},{5,7},{6,4},{7,5},{8,10},{9,11},{10,... | collective-permute-start | bytes 786440 | tf_op jit(solution)/shard_map/ppermute | solution.py:27
  11.0 54.2 %collective-permute-start.6 = (bf16[1024,384]{1,0:T(8,128)(2,1)S(1)}, bf16[1024,384]{1,0:T(8,128)(2,1)S(1)}, u32[]{:S(2)}, u32[]{:S(2)}) collective-permute-start(bf16[1024,384]{1,0:T(8,128)(2,1)S(1)} %convolution_convert_fusion), channel_id=1, source_target_pairs={{0,2},{1,3},{2,0},{3,1},{4,6},{5,7},{6,4},{7,5},{8,10},{9,11},{10,... | collective-permute-start | bytes 2359304 | tf_op jit(solution)/shard_map/ppermute | solution.py:27
  20.9 58.5 %collective-permute-start.13 = (f32[2048,128]{1,0:T(8,128)S(1)}, f32[2048,128]{1,0:T(8,128)S(1)}, u32[]{:S(2)}, u32[]{:S(2)}) collective-permute-start(f32[2048,128]{1,0:T(8,128)S(1)} %get-tuple-element.49), channel_id=1, source_target_pairs={{0,64},{1,5},{2,66},{3,7},{4,68},{5,9},{6,70},{7,11},{8,72},{9,13}... | collective-permute-start | bytes 3145736 | tf_op jit(solution)/shard_map/ppermute | solution.py:27
  36.1 45.4 %collective-permute-start.14 = (f32[2048,128]{1,0:T(8,128)S(1)}, f32[2048,128]{1,0:T(8,128)S(1)}, u32[]{:S(2)}, u32[]{:S(2)}) collective-permute-start(f32[2048,128]{1,0:T(8,128)S(1)} %get-tuple-element.50), channel_id=1, source_target_pairs={{0,128},{1,9},{2,130},{3,11},{4,132},{5,13},{6,134},{7,15},{8,136}... | collective-permute-start | bytes 3145736 | tf_op jit(solution)/shard_map/ppermute | solution.py:27
  39.1 42.3 %collective-permute-start.15 = (f32[2048,128]{1,0:T(8,128)S(1)}, f32[2048,128]{1,0:T(8,128)S(1)}, u32[]{:S(2)}, u32[]{:S(2)}) collective-permute-start(f32[2048,128]{1,0:T(8,128)S(1)} %get-tuple-element.51), channel_id=1, source_target_pairs={{0,192},{1,13},{2,194},{3,15},{4,196},{5,1},{6,198},{7,3},{8,200},... | collective-permute-start | bytes 3145736 | tf_op jit(solution)/shard_map/ppermute | solution.py:27
  45.0 23.3 %collective-permute-start.16 = (f32[640,128]{1,0:T(8,128)S(1)}, f32[640,128]{1,0:T(8,128)S(1)}, u32[]{:S(2)}, u32[]{:S(2)}) collective-permute-start(f32[640,128]{1,0:T(8,128)S(1)} %get-tuple-element.52), channel_id=1, source_target_pairs={{0,64},{1,5},{2,66},{3,7},{4,68},{5,9},{6,70},{7,11},{8,72},{9,13}... | collective-permute-start | bytes 983048 | tf_op jit(solution)/shard_map/ppermute | solution.py:27
  65.2 8.6 %collective-permute-start.17 = (f32[640,128]{1,0:T(8,128)S(1)}, f32[640,128]{1,0:T(8,128)S(1)}, u32[]{:S(2)}, u32[]{:S(2)}) collective-permute-start(f32[640,128]{1,0:T(8,128)S(1)} %get-tuple-element.53), channel_id=1, source_target_pairs={{0,128},{1,9},{2,130},{3,11},{4,132},{5,13},{6,134},{7,15},{8,136}... | collective-permute-start | bytes 983048 | tf_op jit(solution)/shard_map/ppermute | solution.py:27
  68.2 9.2 %collective-permute-start.18 = (f32[640,128]{1,0:T(8,128)S(1)}, f32[640,128]{1,0:T(8,128)S(1)}, u32[]{:S(2)}, u32[]{:S(2)}) collective-permute-start(f32[640,128]{1,0:T(8,128)S(1)} %get-tuple-element.54), channel_id=1, source_target_pairs={{0,192},{1,13},{2,194},{3,15},{4,196},{5,1},{6,198},{7,3},{8,200},... | collective-permute-start | bytes 983048 | tf_op jit(solution)/shard_map/ppermute | solution.py:27
  73.8 37.0 %collective-permute-start.7 = (f32[1536,128]{1,0:T(8,128)S(1)}, f32[1536,128]{1,0:T(8,128)S(1)}, u32[]{:S(2)}, u32[]{:S(2)}) collective-permute-start(f32[1536,128]{1,0:T(8,128)S(1)} %get-tuple-element.41), channel_id=1, source_target_pairs={{0,64},{1,5},{2,66},{3,7},{4,68},{5,9},{6,70},{7,11},{8,72},{9,13}... | collective-permute-start | bytes 2359304 | tf_op jit(solution)/shard_map/ppermute | solution.py:27
  77.4 33.3 %collective-permute-start.8 = (f32[1536,128]{1,0:T(8,128)}, f32[1536,128]{1,0:T(8,128)S(1)}, u32[]{:S(2)}, u32[]{:S(2)}) collective-permute-start(f32[1536,128]{1,0:T(8,128)} %get-tuple-element.42), channel_id=1, source_target_pairs={{0,128},{1,9},{2,130},{3,11},{4,132},{5,13},{6,134},{7,15},{8,136}... | collective-permute-start | bytes 2359304 | tf_op jit(solution)/shard_map/ppermute | solution.py:27
  79.4 31.3 %collective-permute-start.9 = (f32[1536,128]{1,0:T(8,128)}, f32[1536,128]{1,0:T(8,128)S(1)}, u32[]{:S(2)}, u32[]{:S(2)}) collective-permute-start(f32[1536,128]{1,0:T(8,128)} %get-tuple-element.43), channel_id=1, source_target_pairs={{0,192},{1,13},{2,194},{3,15},{4,196},{5,1},{6,198},{7,3},{8,200},... | collective-permute-start | bytes 2359304 | tf_op jit(solution)/shard_map/ppermute | solution.py:27
  82.3 13.5 %collective-permute-start.19 = (f32[672,128]{1,0:T(8,128)S(1)}, f32[672,128]{1,0:T(8,128)S(1)}, u32[]{:S(2)}, u32[]{:S(2)}) collective-permute-start(f32[672,128]{1,0:T(8,128)S(1)} %get-tuple-element.56), channel_id=1, source_target_pairs={{0,4},{1,65},{2,6},{3,67},{4,8},{5,69},{6,10},{7,71},{8,12},{9,73}... | collective-permute-start | bytes 1032200 | tf_op jit(solution)/shard_map/ppermute | solution.py:27
  83.9 17.7 %collective-permute-start.20 = (f32[672,128]{1,0:T(8,128)S(1)}, f32[672,128]{1,0:T(8,128)S(1)}, u32[]{:S(2)}, u32[]{:S(2)}) collective-permute-start(f32[672,128]{1,0:T(8,128)S(1)} %get-tuple-element.57), channel_id=1, source_target_pairs={{0,8},{1,129},{2,10},{3,131},{4,12},{5,133},{6,14},{7,135},{8,0},{... | collective-permute-start | bytes 1032200 | tf_op jit(solution)/shard_map/ppermute | solution.py:27
  95.8 8.7 %collective-permute-start.21 = (f32[672,128]{1,0:T(8,128)S(1)}, f32[672,128]{1,0:T(8,128)S(1)}, u32[]{:S(2)}, u32[]{:S(2)}) collective-permute-start(f32[672,128]{1,0:T(8,128)S(1)} %get-tuple-element.58), channel_id=1, source_target_pairs={{0,12},{1,193},{2,14},{3,195},{4,0},{5,197},{6,2},{7,199},{8,4},{9... | collective-permute-start | bytes 1032200 | tf_op jit(solution)/shard_map/ppermute | solution.py:27
  105.1 11.7 %collective-permute-start.22 = (f32[168,128]{1,0:T(8,128)S(1)}, f32[168,128]{1,0:T(8,128)}, u32[]{:S(2)}, u32[]{:S(2)}) collective-permute-start(f32[168,128]{1,0:T(8,128)S(1)} %get-tuple-element.60), channel_id=1, source_target_pairs={{0,16},{1,17},{2,18},{3,19},{4,20},{5,21},{6,22},{7,23},{8,24},{9,... | collective-permute-start | bytes 258056 | tf_op jit(solution)/shard_map/ppermute | solution.py:27
  105.2 14.1 %collective-permute-start.23 = (f32[168,128]{1,0:T(8,128)S(1)}, f32[168,128]{1,0:T(8,128)}, u32[]{:S(2)}, u32[]{:S(2)}) collective-permute-start(f32[168,128]{1,0:T(8,128)S(1)} %get-tuple-element.61), channel_id=1, source_target_pairs={{0,32},{1,33},{2,34},{3,35},{4,36},{5,37},{6,38},{7,39},{8,40},{9,... | collective-permute-start | bytes 258056 | tf_op jit(solution)/shard_map/ppermute | solution.py:27
  110.8 8.6 %collective-permute-start.24 = (f32[168,128]{1,0:T(8,128)S(1)}, f32[168,128]{1,0:T(8,128)}, u32[]{:S(2)}, u32[]{:S(2)}) collective-permute-start(f32[168,128]{1,0:T(8,128)S(1)} %get-tuple-element.62), channel_id=1, source_target_pairs={{0,48},{1,49},{2,50},{3,51},{4,52},{5,53},{6,54},{7,55},{8,56},{9,... | collective-permute-start | bytes 258056 | tf_op jit(solution)/shard_map/ppermute | solution.py:27
  111.5 8.9 %collective-permute-start.10 = (f32[384,128]{1,0:T(8,128)S(1)}, f32[384,128]{1,0:T(8,128)S(1)}, u32[]{:S(2)}, u32[]{:S(2)}) collective-permute-start(f32[384,128]{1,0:T(8,128)S(1)} %get-tuple-element.45), channel_id=1, source_target_pairs={{0,4},{1,65},{2,6},{3,67},{4,8},{5,69},{6,10},{7,71},{8,12},{9,73}... | collective-permute-start | bytes 589832 | tf_op jit(solution)/shard_map/ppermute | solution.py:27
  114.6 7.8 %collective-permute-start.11 = (f32[384,128]{1,0:T(8,128)S(1)}, f32[384,128]{1,0:T(8,128)S(1)}, u32[]{:S(2)}, u32[]{:S(2)}) collective-permute-start(f32[384,128]{1,0:T(8,128)S(1)} %get-tuple-element.46), channel_id=1, source_target_pairs={{0,8},{1,129},{2,10},{3,131},{4,12},{5,133},{6,14},{7,135},{8,0},{... | collective-permute-start | bytes 589832 | tf_op jit(solution)/shard_map/ppermute | solution.py:27
  116.8 5.7 %collective-permute-start.12 = (f32[384,128]{1,0:T(8,128)S(1)}, f32[384,128]{1,0:T(8,128)S(1)}, u32[]{:S(2)}, u32[]{:S(2)}) collective-permute-start(f32[384,128]{1,0:T(8,128)S(1)} %get-tuple-element.47), channel_id=1, source_target_pairs={{0,12},{1,193},{2,14},{3,195},{4,0},{5,197},{6,2},{7,199},{8,4},{9... | collective-permute-start | bytes 589832 | tf_op jit(solution)/shard_map/ppermute | solution.py:27
  125.4 5.0 %collective-permute-start.26 = (f32[104,128]{1,0:T(8,128)S(1)}, f32[104,128]{1,0:T(8,128)S(1)}, u32[]{:S(2)}, u32[]{:S(2)}) collective-permute-start(f32[104,128]{1,0:T(8,128)S(1)} %get-tuple-element.65), channel_id=1, source_target_pairs={{0,32},{1,33},{2,34},{3,35},{4,36},{5,37},{6,38},{7,39},{8,40},{9,... | collective-permute-start | bytes 159752 | tf_op jit(solution)/shard_map/ppermute | solution.py:27
  131.4 9.1 %collective-permute-start.28 = (f32[32,128]{1,0:T(8,128)S(1)}, f32[32,128]{1,0:T(8,128)S(1)}, u32[]{:S(2)}, u32[]{:S(2)}) collective-permute-start(f32[32,128]{1,0:T(8,128)S(1)} %pad_maximum_fusion.1), channel_id=1, source_target_pairs={{0,64},{1,5},{2,66},{3,7},{4,68},{5,9},{6,70},{7,11},{8,72},{9,13}... | collective-permute-start | bytes 49160 | tf_op jit(solution)/shard_map/ppermute | solution.py:27
  132.8 7.7 %collective-permute-start.29 = (f32[32,128]{1,0:T(8,128)S(1)}, f32[32,128]{1,0:T(8,128)S(1)}, u32[]{:S(2)}, u32[]{:S(2)}) collective-permute-start(f32[32,128]{1,0:T(8,128)S(1)} %pad_maximum_fusion.1), channel_id=1, source_target_pairs={{0,128},{1,9},{2,130},{3,11},{4,132},{5,13},{6,134},{7,15},{8,136}... | collective-permute-start | bytes 49160 | tf_op jit(solution)/shard_map/ppermute | solution.py:27
  134.5 6.1 %collective-permute-start.30 = (f32[32,128]{1,0:T(8,128)S(1)}, f32[32,128]{1,0:T(8,128)S(1)}, u32[]{:S(2)}, u32[]{:S(2)}) collective-permute-start(f32[32,128]{1,0:T(8,128)S(1)} %pad_maximum_fusion.1), channel_id=1, source_target_pairs={{0,192},{1,13},{2,194},{3,15},{4,196},{5,1},{6,198},{7,3},{8,200},... | collective-permute-start | bytes 49160 | tf_op jit(solution)/shard_map/ppermute | solution.py:27
  137.0 10.5 %collective-permute-start.34 = (f32[128,128]{1,0:T(8,128)S(1)}, f32[128,128]{1,0:T(8,128)S(1)}, u32[]{:S(2)}, u32[]{:S(2)}) collective-permute-start(f32[128,128]{1,0:T(8,128)S(1)} %get-tuple-element.69), channel_id=1, source_target_pairs={{0,2},{1,3},{2,130},{3,131},{4,6},{5,7},{6,134},{7,135},{8,10},{9,... | collective-permute-start | bytes 196616 | tf_op jit(solution)/shard_map/ppermute | solution.py:27
  139.8 7.7 %collective-permute-start.35 = (f32[128,128]{1,0:T(8,128)S(1)}, f32[128,128]{1,0:T(8,128)S(1)}, u32[]{:S(2)}, u32[]{:S(2)}) collective-permute-start(f32[128,128]{1,0:T(8,128)S(1)} %get-tuple-element.71.cross), channel_id=1, source_target_pairs={{3,66},{7,70},{11,74},{15,78},{19,82},{23,86},{27,90},{31,94},{35,... | collective-permute-start | bytes 196616 | tf_op jit(solution)/shard_map/ppermute | solution.py:27
  140.6 8.2 %collective-permute-start.31 = (f32[128,128]{1,0:T(8,128)S(1)}, f32[128,128]{1,0:T(8,128)S(1)}, u32[]{:S(2)}, u32[]{:S(2)}) collective-permute-start(f32[128,128]{1,0:T(8,128)S(1)} %constant_dynamic-update-slice_fusion.a), channel_id=1, source_target_pairs={{0,4},{1,65},{2,6},{3,67},{4,8},{5,69},{6,10},{7,71},{8,12},{9,73}... | collective-permute-start | bytes 196616 | tf_op jit(solution)/shard_map/ppermute | solution.py:27
  142.6 6.2 %collective-permute-start.32 = (f32[128,128]{1,0:T(8,128)S(1)}, f32[128,128]{1,0:T(8,128)S(1)}, u32[]{:S(2)}, u32[]{:S(2)}) collective-permute-start(f32[128,128]{1,0:T(8,128)S(1)} %constant_dynamic-update-slice_fusion.a), channel_id=1, source_target_pairs={{0,8},{1,129},{2,10},{3,131},{4,12},{5,133},{6,14},{7,135},{8,0},{... | collective-permute-start | bytes 196616 | tf_op jit(solution)/shard_map/ppermute | solution.py:27
  (7 other events, 21.6 us)

commit v2 on v1

--- a/solution.py
+++ b/solution.py
@@ -165,27 +165,29 @@
                 start += size
 
 
-def last_kernel(size, scalars, a, b, c, d, *rest):
+def last_kernel(scalars, a, b, c, d, e, f, g, h, *outs):
     zl = scalars[2]
-    more, outs = rest[:-4], rest[-4:]
     for j, out in enumerate(outs):
-        at = rows_at(lax.rem(zl + j, 4), size, 0, size)
-        out[:size] = (a[at] + b[at]) + (c[at] + d[at])
-        for piece in more:
-            out[size:] = piece[...]
+        i = lax.rem(zl + j, 4)
+        at = rows_at(i, 168, 0, 160)
+        out[:160] = (a[at] + b[at]) + (c[at] + d[at])
+        for slab in range(4):
+            at = pl.ds(168 * slab + 160, 8)
+            out[160 + 8 * slab : 168 + 8 * slab] = (a[at] + b[at]) + (c[at] + d[at])
+        at = rows_at(i, 96, 0, 96)
+        out[192:] = (e[at] + f[at]) + (g[at] + h[at])
 
 
 def latent_kernel(scale, scalars, a, b, c, d, out):
-    x, y, zl, core = scalars[0], scalars[1], scalars[2], scalars[4]
+    x, y, core = scalars[0], scalars[1], scalars[4]
     is0 = core == 0
     for j2, ref in enumerate((a, b, c, d)):
         for j1 in range(4):
-            for jz in range(4):
+            for zb in range(4):
                 xb = lax.rem(x + 4 - jnp.where(is0, j1, j2), 4)
                 yb = lax.rem(y + 4 - jnp.where(is0, j2, j1), 4)
-                zb = lax.rem(zl + 4 - jz, 4)
                 to = rows_at(16 * xb + 4 * zb + yb, 8, 0, 8)
-                at = 32 * j1 + 8 * jz
+                at = 32 * j1 + 8 * zb
                 out[to, :] = ref[at : at + 8, :] * scale
 
 
@@ -300,10 +302,6 @@
         kernel = functools.partial(middle_kernel, sizes)
         return sums_call(kernel, [(4 * sum(sizes), 128)] * 4, after(scalars, gate), *parts)
 
-    def last(size, *parts):
-        rows = size + sum(p.shape[0] for p in parts[4:])
-        return sums_call(functools.partial(last_kernel, size), [(rows, 128)] * 4, scalars, *parts)
-
     own = blocks_call(
         own_kernel, 16 * 128, scalars, grad_key, key_other, grad_value, value_other
     )
@@ -322,15 +320,11 @@
     c0 = middle((128, 40), *own, *c0, gate=c1[0])
     c1 = exchange(c1, first)
     c0 = exchange(c0, second)
-    c0 = exchange(last(168, *c0), along_z)
-    c0 = (c0[0] + c0[1]) + (c0[2] + c0[3])
-    own = c0[:128]
-    c = middle((96,), *c1, gate=gate)
-    c = exchange(c, second)
-    c = exchange(last(96, *c, c0[160:]), along_z)
-    pieces = jnp.concatenate([part[96:] for part in c], axis=0)
-    ends = (c[0][:96] + c[1][:96]) + (c[2][:96] + c[3][:96])
-    crossed = jnp.concatenate([c0[128:160], ends], axis=0)
+    c = exchange(middle((96,), *c1, gate=gate), second)
+    c = exchange(sums_call(last_kernel, [(288, 128)] * 4, scalars, *c0, *c), along_z)
+    c = (c[0] + c[1]) + (c[2] + c[3])
+    own, pieces = c[:128], c[160:192]
+    crossed = jnp.concatenate([c[128:160], c[192:]], axis=0)
     pieces = jnp.concatenate(exchange([pieces] * 4, first), axis=0)
     moved = move(jnp.where(x // 2 == zh, crossed, own), homeward)
     turned = move(crossed, sideways)

time: 152 us -> 179 us (1.18)
  waiting for transfers between devices: 61.4 us -> 101 us
  starting transfers between devices: 68.1 us -> 57.3 us
    ppermute x36 -> x33, waiting for transfers between devices: 61.4 us -> 101 us  [move(): return lax.ppermute(values, AXES, pairs)]
    ppermute x36 -> x33, starting transfers between devices: 68.1 us -> 57.3 us  [move(): return lax.ppermute(values, AXES, pairs)]
    pallas_call x6 -> x5, Pallas kernels: 5.37 us -> 4.75 us  [sums_call(): pl.pallas_call(kernel, out_shape=outs, in_specs=[SMEM] * len(head) + [VME...]
  transfers between devices with their start and end apart: 36 -> 33, of which waited for: 14 -> 11; matrix products, arithmetic and copies ran while one was open for 3% -> 2% of each run, Pallas kernels for 9% -> 5%
where the time goes in v2:
time: 179 us
  waiting for transfers between devices  101 us (56%)
  starting transfers between devices  57.3 us (32%)
  Pallas kernels  15.1 us (8%)
  matrix products  3.47 us (2%)
    ppermute x33, waiting for transfers between devices, move(): return lax.ppermute(values, AXES, pairs)  101 us
    ppermute x33, starting transfers between devices, move(): return lax.ppermute(values, AXES, pairs)  57.3 us
    pallas_call x3, Pallas kernels, blocks_call(): pl.pallas_call(kernel, out_shape=outs, in_specs=[SMEM] + [VMEM] * len(ope...  10.4 us
    pallas_call x5, Pallas kernels, sums_call(): pl.pallas_call(kernel, out_shape=outs, in_specs=[SMEM] * len(head) + [VME...  4.75 us
  transfers between devices with their start and end apart: 33, of which 11 were waited for; matrix products, arithmetic and copies ran while one was open for 2% of the time, Pallas kernels for 5%

profile of v2, /device:TPU:32, one launch (start us, length us, event | category | flops | bytes accessed | tf_op | source)
XLA Modules:
  0.0 178.6 jit_solution(15511536329221236472)
XLA Ops:
  1.2 6.3 %collective-permute-start.3 = (bf16[1024,128]{1,0:T(8,128)(2,1)}, bf16[1024,128]{1,0:T(8,128)(2,1)S(1)}, u32[]{:S(2)}, u32[]{:S(2)}) collective-permute-start(bf16[1024,128]{1,0:T(8,128)(2,1)} %rest_0_.1), channel_id=1, source_target_pairs={{0,2},{1,3},{2,0},{3,1},{4,6},{5,7},{6,4},{7,5},{8,10},{9,11},{10,... | collective-permute-start | bytes 786440 | tf_op jit(solution)/shard_map/ppermute | solution.py:27
  7.6 3.0 %convolution_convert_fusion = bf16[1024,384]{1,0:T(8,128)(2,1)} fusion(bf16[1024,512]{1,0:T(8,128)(2,1)} %vm.1, bf16[1024,512]{1,0:T(8,128)(2,1)} %km.1, pred[]{:T(512)S(6)} %eq.49, s32[384]{0:T(512)S(1)} %slice.19), kind=kOutput, calls=%fused_computation | convolution fusion | flops 403767296 | bytes 2885121 | tf_op jit(solution)/shard_map/dot_general | solution.py:288
  11.9 9.0 %collective-permute-done.3.rest_2_ = bf16[1024,128]{1,0:T(8,128)(2,1)S(1)} collective-permute-done((bf16[1024,128]{1,0:T(8,128)(2,1)}, bf16[1024,128]{1,0:T(8,128)(2,1)S(1)}, u32[]{:S(2)}, u32[]{:S(2)}) %collective-permute-start.3) | collective-permute-done | bytes 262176 | tf_op jit(solution)/shard_map/ppermute | solution.py:27
  20.9 8.5 %collective-permute-start.5 = (bf16[1024,128]{1,0:T(8,128)(2,1)S(1)}, bf16[1024,128]{1,0:T(8,128)(2,1)S(1)}, u32[]{:S(2)}, u32[]{:S(2)}) collective-permute-start(bf16[1024,128]{1,0:T(8,128)(2,1)S(1)} %convolution_convert_fusion.1), channel_id=1, source_target_pairs={{0,2},{1,3},{2,0},{3,1},{4,6},{5,7},{6,4},{7,5},{8,10},{9,11},{10,... | collective-permute-start | bytes 786440 | tf_op jit(solution)/shard_map/ppermute | solution.py:27
  29.4 3.9 %shard_map.58 = (f32[2048,128]{1,0:T(8,128)S(1)}, f32[2048,128]{1,0:T(8,128)S(1)}, f32[2048,128]{1,0:T(8,128)S(1)}, f32[2048,128]{1,0:T(8,128)S(1)}) custom-call(s32[5]{0:T(128)S(1)} %stack.23.scalars, bf16[1024,512]{1,0:T(8,128)(2,1)S(1)} %copy-done, bf16[1024,512]{1,0:T(8,128)(2,1)S(1)} %collective-permute-done.ko, bf16[1024,512]{1,0:T(8,128)(2,1)S(1)} %copy-done.1, ...), custom_call_target="tpu_custom_call" | custom-call | tf_op jit(solution)/shard_map/pallas_call | solution.py:242
  33.5 31.5 %collective-permute-done.5.rest_4_ = bf16[1024,128]{1,0:T(8,128)(2,1)S(1)} collective-permute-done((bf16[1024,128]{1,0:T(8,128)(2,1)S(1)}, bf16[1024,128]{1,0:T(8,128)(2,1)S(1)}, u32[]{:S(2)}, u32[]{:S(2)}) %collective-permute-start.5) | collective-permute-done | bytes 262176 | tf_op jit(solution)/shard_map/ppermute | solution.py:27
  65.0 2.8 %shard_map.59 = (f32[640,128]{1,0:T(8,128)S(1)}, f32[640,128]{1,0:T(8,128)S(1)}, f32[640,128]{1,0:T(8,128)S(1)}, f32[640,128]{1,0:T(8,128)S(1)}) custom-call(s32[5]{0:T(128)S(1)} %stack.23.scalars, bf16[1024,512]{1,0:T(8,128)(2,1)S(1)} %broadcast_select_fusion.2.nm, bf16[1024,512]{1,0:T(8,128)(2,1)S(1)} %broadcast_select_fusion.1.no, ...), custom_call_target="tpu_custom_call" | custom-call | tf_op jit(solution)/shard_map/pallas_call | solution.py:242
  67.8 3.7 %shard_map.60 = (f32[1536,128]{1,0:T(8,128)S(1)}, f32[1536,128]{1,0:T(8,128)S(1)}, f32[1536,128]{1,0:T(8,128)S(1)}, f32[1536,128]{1,0:T(8,128)S(1)}) custom-call(s32[5]{0:T(128)S(1)} %stack.23.scalars, bf16[1024,512]{1,0:T(8,128)(2,1)S(1)} %broadcast_select_fusion.2.nm, bf16[1024,512]{1,0:T(8,128)(2,1)S(1)} %broadcast_select_fusion.1.no, ...), custom_call_target="tpu_custom_call" | custom-call | tf_op jit(solution)/shard_map/pallas_call | solution.py:242
  71.4 1.6 collective-permute-start.16
  73.0 1.5 collective-permute-start.10
  74.5 1.7 collective-permute-start.17
  76.2 2.2 %collective-permute-start.18 = (f32[1536,128]{1,0:T(8,128)S(1)}, f32[1536,128]{1,0:T(8,128)S(1)}, u32[]{:S(2)}, u32[]{:S(2)}) collective-permute-start(f32[1536,128]{1,0:T(8,128)S(1)} %get-tuple-element.50), channel_id=1, source_target_pairs={{0,192},{1,13},{2,194},{3,15},{4,196},{5,1},{6,198},{7,3},{8,200},... | collective-permute-start | bytes 2359304 | tf_op jit(solution)/shard_map/ppermute | solution.py:27
  78.4 9.9 %collective-permute-done.10.refs_5_ = f32[640,128]{1,0:T(8,128)S(1)} collective-permute-done((f32[640,128]{1,0:T(8,128)S(1)}, f32[640,128]{1,0:T(8,128)S(1)}, u32[]{:S(2)}, u32[]{:S(2)}) %collective-permute-start.10) | collective-permute-done | bytes 327712 | tf_op jit(solution)/shard_map/ppermute | solution.py:27
  88.2 1.8 %collective-permute-start.8 = (f32[2048,128]{1,0:T(8,128)S(1)}, f32[2048,128]{1,0:T(8,128)S(1)}, u32[]{:S(2)}, u32[]{:S(2)}) collective-permute-start(f32[2048,128]{1,0:T(8,128)S(1)} %get-tuple-element.39), channel_id=1, source_target_pairs={{0,128},{1,9},{2,130},{3,11},{4,132},{5,13},{6,134},{7,15},{8,136}... | collective-permute-start | bytes 3145736 | tf_op jit(solution)/shard_map/ppermute | solution.py:27
  91.2 6.5 %collective-permute-done.17.refs_2_ = f32[1536,128]{1,0:T(8,128)S(1)} collective-permute-done((f32[1536,128]{1,0:T(8,128)S(1)}, f32[1536,128]{1,0:T(8,128)S(1)}, u32[]{:S(2)}, u32[]{:S(2)}) %collective-permute-start.17) | collective-permute-done | bytes 786464 | tf_op jit(solution)/shard_map/ppermute | solution.py:27
  99.3 24.4 %collective-permute-done.11.refs_6_ = f32[640,128]{1,0:T(8,128)S(1)} collective-permute-done((f32[640,128]{1,0:T(8,128)S(1)}, f32[640,128]{1,0:T(8,128)S(1)}, u32[]{:S(2)}, u32[]{:S(2)}) %collective-permute-start.11) | collective-permute-done | bytes 327712 | tf_op jit(solution)/shard_map/ppermute | solution.py:27
  123.7 1.6 collective-permute-start.19
  126.1 1.7 collective-permute-start.13
  127.8 2.8 %collective-permute-start.14 = (f32[672,128]{1,0:T(8,128)S(1)}, f32[672,128]{1,0:T(8,128)S(1)}, u32[]{:S(2)}, u32[]{:S(2)}) collective-permute-start(f32[672,128]{1,0:T(8,128)S(1)} %get-tuple-element.46), channel_id=1, source_target_pairs={{0,8},{1,129},{2,10},{3,131},{4,12},{5,133},{6,14},{7,135},{8,0},{... | collective-permute-start | bytes 1032200 | tf_op jit(solution)/shard_map/ppermute | solution.py:27
  132.3 2.9 %collective-permute-start.21 = (f32[384,128]{1,0:T(8,128)S(1)}, f32[384,128]{1,0:T(8,128)S(1)}, u32[]{:S(2)}, u32[]{:S(2)}) collective-permute-start(f32[384,128]{1,0:T(8,128)S(1)} %get-tuple-element.54), channel_id=1, source_target_pairs={{0,12},{1,193},{2,14},{3,195},{4,0},{5,197},{6,2},{7,199},{8,4},{9... | collective-permute-start | bytes 589832 | tf_op jit(solution)/shard_map/ppermute | solution.py:27
  135.2 6.3 %collective-permute-done.20.g = f32[384,128]{1,0:T(8,128)S(1)} collective-permute-done((f32[384,128]{1,0:T(8,128)S(1)}, f32[384,128]{1,0:T(8,128)S(1)}, u32[]{:S(2)}, u32[]{:S(2)}) %collective-permute-start.20) | collective-permute-done | bytes 196640 | tf_op jit(solution)/shard_map/ppermute | solution.py:27
  141.5 1.9 %collective-permute-done.21.h = f32[384,128]{1,0:T(8,128)S(1)} collective-permute-done((f32[384,128]{1,0:T(8,128)S(1)}, f32[384,128]{1,0:T(8,128)S(1)}, u32[]{:S(2)}, u32[]{:S(2)}) %collective-permute-start.21) | collective-permute-done | bytes 196640 | tf_op jit(solution)/shard_map/ppermute | solution.py:27
  144.2 6.1 %collective-permute-start.23 = (f32[288,128]{1,0:T(8,128)S(1)}, f32[288,128]{1,0:T(8,128)S(1)}, u32[]{:S(2)}, u32[]{:S(2)}) collective-permute-start(f32[288,128]{1,0:T(8,128)S(1)} %get-tuple-element.57), channel_id=1, source_target_pairs={{0,32},{1,33},{2,34},{3,35},{4,36},{5,37},{6,38},{7,39},{8,40},{9,... | collective-permute-start | bytes 442376 | tf_op jit(solution)/shard_map/ppermute | solution.py:27
  150.3 2.3 %collective-permute-done.22 = f32[288,128]{1,0:T(8,128)S(1)} collective-permute-done((f32[288,128]{1,0:T(8,128)S(1)}, f32[288,128]{1,0:T(8,128)S(1)}, u32[]{:S(2)}, u32[]{:S(2)}) %collective-permute-start.22) | collective-permute-done | bytes 147488 | tf_op jit(solution)/shard_map/ppermute | solution.py:27
  152.6 3.7 %collective-permute-done.23 = f32[288,128]{1,0:T(8,128)S(1)} collective-permute-done((f32[288,128]{1,0:T(8,128)S(1)}, f32[288,128]{1,0:T(8,128)S(1)}, u32[]{:S(2)}, u32[]{:S(2)}) %collective-permute-start.23) | collective-permute-done | bytes 147488 | tf_op jit(solution)/shard_map/ppermute | solution.py:27
  156.4 3.8 %collective-permute-done.24 = f32[288,128]{1,0:T(8,128)S(1)} collective-permute-done((f32[288,128]{1,0:T(8,128)S(1)}, f32[288,128]{1,0:T(8,128)S(1)}, u32[]{:S(2)}, u32[]{:S(2)}) %collective-permute-start.24) | collective-permute-done | bytes 147488 | tf_op jit(solution)/shard_map/ppermute | solution.py:27
  160.2 2.0 %collective-permute-start.25 = (f32[32,128]{1,0:T(8,128)S(1)}, f32[32,128]{1,0:T(8,128)S(1)}, u32[]{:S(2)}, u32[]{:S(2)}) collective-permute-start(f32[32,128]{1,0:T(8,128)S(1)} %get-tuple-element.64), channel_id=1, source_target_pairs={{0,64},{1,5},{2,66},{3,7},{4,68},{5,9},{6,70},{7,11},{8,72},{9,13}... | collective-permute-start | bytes 49160 | tf_op jit(solution)/shard_map/ppermute | solution.py:27
  162.1 2.4 %collective-permute-start.26 = (f32[32,128]{1,0:T(8,128)S(1)}, f32[32,128]{1,0:T(8,128)S(1)}, u32[]{:S(2)}, u32[]{:S(2)}) collective-permute-start(f32[32,128]{1,0:T(8,128)S(1)} %get-tuple-element.64), channel_id=1, source_target_pairs={{0,128},{1,9},{2,130},{3,11},{4,132},{5,13},{6,134},{7,15},{8,136}... | collective-permute-start | bytes 49160 | tf_op jit(solution)/shard_map/ppermute | solution.py:27
  166.0 2.5 %collective-permute-start.31 = (f32[128,128]{1,0:T(8,128)S(1)}, f32[128,128]{1,0:T(8,128)S(1)}, u32[]{:S(2)}, u32[]{:S(2)}) collective-permute-start(f32[128,128]{1,0:T(8,128)S(1)} %get-tuple-element.61), channel_id=1, source_target_pairs={{0,2},{1,3},{2,130},{3,131},{4,6},{5,7},{6,134},{7,135},{8,10},{9,... | collective-permute-start | bytes 196616 | tf_op jit(solution)/shard_map/ppermute | solution.py:27
  169.2 2.3 %collective-permute-start.28 = (f32[128,128]{1,0:T(8,128)S(1)}, f32[128,128]{1,0:T(8,128)S(1)}, u32[]{:S(2)}, u32[]{:S(2)}) collective-permute-start(f32[128,128]{1,0:T(8,128)S(1)} %pad_maximum_fusion.a), channel_id=1, source_target_pairs={{0,4},{1,65},{2,6},{3,67},{4,8},{5,69},{6,10},{7,71},{8,12},{9,73}... | collective-permute-start | bytes 196616 | tf_op jit(solution)/shard_map/ppermute | solution.py:27
  171.5 1.5 collective-permute-start.29
  173.0 1.5 collective-permute-start.30
  (67 shorter events, 14.3 us)
Async XLA Ops:
  0.6 28.7 %collective-permute-start = (bf16[1024,512]{1,0:T(8,128)(2,1)}, bf16[1024,512]{1,0:T(8,128)(2,1)S(1)}, u32[]{:S(2)}, u32[]{:S(2)}) collective-permute-start(bf16[1024,512]{1,0:T(8,128)(2,1)} %km.1), channel_id=1, source_target_pairs={{0,1},{1,0},{2,3},{3,2},{4,5},{5,4},{6,7},{7,6},{8,9},{9,8},{10,11... | collective-permute-start | bytes 3145736 | tf_op jit(solution)/shard_map/ppermute | solution.py:27
  0.7 28.6 %collective-permute-start.1 = (bf16[1024,512]{1,0:T(8,128)(2,1)}, bf16[1024,512]{1,0:T(8,128)(2,1)}, u32[]{:S(2)}, u32[]{:S(2)}) collective-permute-start(bf16[1024,512]{1,0:T(8,128)(2,1)} %vm.1), channel_id=1, source_target_pairs={{0,1},{1,0},{2,3},{3,2},{4,5},{5,4},{6,7},{7,6},{8,9},{9,8},{10,11... | collective-permute-start | bytes 3145736 | tf_op jit(solution)/shard_map/ppermute | solution.py:27
  1.2 19.6 %collective-permute-start.3 = (bf16[1024,128]{1,0:T(8,128)(2,1)}, bf16[1024,128]{1,0:T(8,128)(2,1)S(1)}, u32[]{:S(2)}, u32[]{:S(2)}) collective-permute-start(bf16[1024,128]{1,0:T(8,128)(2,1)} %rest_0_.1), channel_id=1, source_target_pairs={{0,2},{1,3},{2,0},{3,1},{4,6},{5,7},{6,4},{7,5},{8,10},{9,11},{10,... | collective-permute-start | bytes 786440 | tf_op jit(solution)/shard_map/ppermute | solution.py:27
  7.5 57.4 %collective-permute-start.2 = (bf16[1024,128]{1,0:T(8,128)(2,1)}, bf16[1024,128]{1,0:T(8,128)(2,1)}, u32[]{:S(2)}, u32[]{:S(2)}) collective-permute-start(bf16[1024,128]{1,0:T(8,128)(2,1)} %rest_0_.1), channel_id=1, source_target_pairs={{0,1},{1,0},{2,3},{3,2},{4,5},{5,4},{6,7},{7,6},{8,9},{9,8},{10,11... | collective-permute-start | bytes 786440 | tf_op jit(solution)/shard_map/ppermute | solution.py:27
  10.6 57.2 %collective-permute-start.6 = (bf16[1024,384]{1,0:T(8,128)(2,1)}, bf16[1024,384]{1,0:T(8,128)(2,1)}, u32[]{:S(2)}, u32[]{:S(2)}) collective-permute-start(bf16[1024,384]{1,0:T(8,128)(2,1)} %convolution_convert_fusion), channel_id=1, source_target_pairs={{0,2},{1,3},{2,0},{3,1},{4,6},{5,7},{6,4},{7,5},{8,10},{9,11},{10,... | collective-permute-start | bytes 2359304 | tf_op jit(solution)/shard_map/ppermute | solution.py:27
  20.9 44.1 %collective-permute-start.5 = (bf16[1024,128]{1,0:T(8,128)(2,1)S(1)}, bf16[1024,128]{1,0:T(8,128)(2,1)S(1)}, u32[]{:S(2)}, u32[]{:S(2)}) collective-permute-start(bf16[1024,128]{1,0:T(8,128)(2,1)S(1)} %convolution_convert_fusion.1), channel_id=1, source_target_pairs={{0,2},{1,3},{2,0},{3,1},{4,6},{5,7},{6,4},{7,5},{8,10},{9,11},{10,... | collective-permute-start | bytes 786440 | tf_op jit(solution)/shard_map/ppermute | solution.py:27
  29.4 35.6 %collective-permute-start.4 = (bf16[1024,128]{1,0:T(8,128)(2,1)S(1)}, bf16[1024,128]{1,0:T(8,128)(2,1)S(1)}, u32[]{:S(2)}, u32[]{:S(2)}) collective-permute-start(bf16[1024,128]{1,0:T(8,128)(2,1)S(1)} %collective-permute-done.3.rest_2_), channel_id=1, source_target_pairs={{0,1},{1,0},{2,3},{3,2},{4,5},{5,4},{6,7},{7,6},{8,9},{9,8},{10,11... | collective-permute-start | bytes 786440 | tf_op jit(solution)/shard_map/ppermute | solution.py:27
  71.4 18.6 %collective-permute-start.16 = (f32[1536,128]{1,0:T(8,128)S(1)}, f32[1536,128]{1,0:T(8,128)S(1)}, u32[]{:S(2)}, u32[]{:S(2)}) collective-permute-start(f32[1536,128]{1,0:T(8,128)S(1)} %get-tuple-element.48), channel_id=1, source_target_pairs={{0,64},{1,5},{2,66},{3,7},{4,68},{5,9},{6,70},{7,11},{8,72},{9,13}... | collective-permute-start | bytes 2359304 | tf_op jit(solution)/shard_map/ppermute | solution.py:27
  73.0 15.2 %collective-permute-start.10 = (f32[640,128]{1,0:T(8,128)S(1)}, f32[640,128]{1,0:T(8,128)S(1)}, u32[]{:S(2)}, u32[]{:S(2)}) collective-permute-start(f32[640,128]{1,0:T(8,128)S(1)} %get-tuple-element.41), channel_id=1, source_target_pairs={{0,64},{1,5},{2,66},{3,7},{4,68},{5,9},{6,70},{7,11},{8,72},{9,13}... | collective-permute-start | bytes 983048 | tf_op jit(solution)/shard_map/ppermute | solution.py:27
  74.5 23.2 %collective-permute-start.17 = (f32[1536,128]{1,0:T(8,128)S(1)}, f32[1536,128]{1,0:T(8,128)S(1)}, u32[]{:S(2)}, u32[]{:S(2)}) collective-permute-start(f32[1536,128]{1,0:T(8,128)S(1)} %get-tuple-element.49), channel_id=1, source_target_pairs={{0,128},{1,9},{2,130},{3,11},{4,132},{5,13},{6,134},{7,15},{8,136}... | collective-permute-start | bytes 2359304 | tf_op jit(solution)/shard_map/ppermute | solution.py:27
  76.2 22.3 %collective-permute-start.18 = (f32[1536,128]{1,0:T(8,128)S(1)}, f32[1536,128]{1,0:T(8,128)S(1)}, u32[]{:S(2)}, u32[]{:S(2)}) collective-permute-start(f32[1536,128]{1,0:T(8,128)S(1)} %get-tuple-element.50), channel_id=1, source_target_pairs={{0,192},{1,13},{2,194},{3,15},{4,196},{5,1},{6,198},{7,3},{8,200},... | collective-permute-start | bytes 2359304 | tf_op jit(solution)/shard_map/ppermute | solution.py:27
  78.4 46.9 %collective-permute-start.7 = (f32[2048,128]{1,0:T(8,128)S(1)}, f32[2048,128]{1,0:T(8,128)S(1)}, u32[]{:S(2)}, u32[]{:S(2)}) collective-permute-start(f32[2048,128]{1,0:T(8,128)S(1)} %get-tuple-element.38), channel_id=1, source_target_pairs={{0,64},{1,5},{2,66},{3,7},{4,68},{5,9},{6,70},{7,11},{8,72},{9,13}... | collective-permute-start | bytes 3145736 | tf_op jit(solution)/shard_map/ppermute | solution.py:27
  88.2 37.0 %collective-permute-start.8 = (f32[2048,128]{1,0:T(8,128)S(1)}, f32[2048,128]{1,0:T(8,128)S(1)}, u32[]{:S(2)}, u32[]{:S(2)}) collective-permute-start(f32[2048,128]{1,0:T(8,128)S(1)} %get-tuple-element.39), channel_id=1, source_target_pairs={{0,128},{1,9},{2,130},{3,11},{4,132},{5,13},{6,134},{7,15},{8,136}... | collective-permute-start | bytes 3145736 | tf_op jit(solution)/shard_map/ppermute | solution.py:27
  90.1 35.2 %collective-permute-start.9 = (f32[2048,128]{1,0:T(8,128)S(1)}, f32[2048,128]{1,0:T(8,128)S(1)}, u32[]{:S(2)}, u32[]{:S(2)}) collective-permute-start(f32[2048,128]{1,0:T(8,128)S(1)} %get-tuple-element.40), channel_id=1, source_target_pairs={{0,192},{1,13},{2,194},{3,15},{4,196},{5,1},{6,198},{7,3},{8,200},... | collective-permute-start | bytes 3145736 | tf_op jit(solution)/shard_map/ppermute | solution.py:27
  97.7 25.9 %collective-permute-start.11 = (f32[640,128]{1,0:T(8,128)S(1)}, f32[640,128]{1,0:T(8,128)S(1)}, u32[]{:S(2)}, u32[]{:S(2)}) collective-permute-start(f32[640,128]{1,0:T(8,128)S(1)} %get-tuple-element.42), channel_id=1, source_target_pairs={{0,128},{1,9},{2,130},{3,11},{4,132},{5,13},{6,134},{7,15},{8,136}... | collective-permute-start | bytes 983048 | tf_op jit(solution)/shard_map/ppermute | solution.py:27
  98.6 26.7 %collective-permute-start.12 = (f32[640,128]{1,0:T(8,128)S(1)}, f32[640,128]{1,0:T(8,128)S(1)}, u32[]{:S(2)}, u32[]{:S(2)}) collective-permute-start(f32[640,128]{1,0:T(8,128)S(1)} %get-tuple-element.43), channel_id=1, source_target_pairs={{0,192},{1,13},{2,194},{3,15},{4,196},{5,1},{6,198},{7,3},{8,200},... | collective-permute-start | bytes 983048 | tf_op jit(solution)/shard_map/ppermute | solution.py:27
  123.7 8.7 %collective-permute-start.19 = (f32[384,128]{1,0:T(8,128)S(1)}, f32[384,128]{1,0:T(8,128)S(1)}, u32[]{:S(2)}, u32[]{:S(2)}) collective-permute-start(f32[384,128]{1,0:T(8,128)S(1)} %get-tuple-element.52), channel_id=1, source_target_pairs={{0,4},{1,65},{2,6},{3,67},{4,8},{5,69},{6,10},{7,71},{8,12},{9,73}... | collective-permute-start | bytes 589832 | tf_op jit(solution)/shard_map/ppermute | solution.py:27
  126.1 17.3 %collective-permute-start.13 = (f32[672,128]{1,0:T(8,128)S(1)}, f32[672,128]{1,0:T(8,128)S(1)}, u32[]{:S(2)}, u32[]{:S(2)}) collective-permute-start(f32[672,128]{1,0:T(8,128)S(1)} %get-tuple-element.45), channel_id=1, source_target_pairs={{0,4},{1,65},{2,6},{3,67},{4,8},{5,69},{6,10},{7,71},{8,12},{9,73}... | collective-permute-start | bytes 1032200 | tf_op jit(solution)/shard_map/ppermute | solution.py:27
  127.8 15.7 %collective-permute-start.14 = (f32[672,128]{1,0:T(8,128)S(1)}, f32[672,128]{1,0:T(8,128)S(1)}, u32[]{:S(2)}, u32[]{:S(2)}) collective-permute-start(f32[672,128]{1,0:T(8,128)S(1)} %get-tuple-element.46), channel_id=1, source_target_pairs={{0,8},{1,129},{2,10},{3,131},{4,12},{5,133},{6,14},{7,135},{8,0},{... | collective-permute-start | bytes 1032200 | tf_op jit(solution)/shard_map/ppermute | solution.py:27
  130.5 12.9 %collective-permute-start.15 = (f32[672,128]{1,0:T(8,128)S(1)}, f32[672,128]{1,0:T(8,128)S(1)}, u32[]{:S(2)}, u32[]{:S(2)}) collective-permute-start(f32[672,128]{1,0:T(8,128)S(1)} %get-tuple-element.47), channel_id=1, source_target_pairs={{0,12},{1,193},{2,14},{3,195},{4,0},{5,197},{6,2},{7,199},{8,4},{9... | collective-permute-start | bytes 1032200 | tf_op jit(solution)/shard_map/ppermute | solution.py:27
  131.9 9.7 %collective-permute-start.20 = (f32[384,128]{1,0:T(8,128)S(1)}, f32[384,128]{1,0:T(8,128)S(1)}, u32[]{:S(2)}, u32[]{:S(2)}) collective-permute-start(f32[384,128]{1,0:T(8,128)S(1)} %get-tuple-element.53), channel_id=1, source_target_pairs={{0,8},{1,129},{2,10},{3,131},{4,12},{5,133},{6,14},{7,135},{8,0},{... | collective-permute-start | bytes 589832 | tf_op jit(solution)/shard_map/ppermute | solution.py:27
  132.3 11.1 %collective-permute-start.21 = (f32[384,128]{1,0:T(8,128)S(1)}, f32[384,128]{1,0:T(8,128)S(1)}, u32[]{:S(2)}, u32[]{:S(2)}) collective-permute-start(f32[384,128]{1,0:T(8,128)S(1)} %get-tuple-element.54), channel_id=1, source_target_pairs={{0,12},{1,193},{2,14},{3,195},{4,0},{5,197},{6,2},{7,199},{8,4},{9... | collective-permute-start | bytes 589832 | tf_op jit(solution)/shard_map/ppermute | solution.py:27
  144.1 8.5 %collective-permute-start.22 = (f32[288,128]{1,0:T(8,128)S(1)}, f32[288,128]{1,0:T(8,128)S(1)}, u32[]{:S(2)}, u32[]{:S(2)}) collective-permute-start(f32[288,128]{1,0:T(8,128)S(1)} %get-tuple-element.56), channel_id=1, source_target_pairs={{0,16},{1,17},{2,18},{3,19},{4,20},{5,21},{6,22},{7,23},{8,24},{9,... | collective-permute-start | bytes 442376 | tf_op jit(solution)/shard_map/ppermute | solution.py:27
  144.2 12.1 %collective-permute-start.23 = (f32[288,128]{1,0:T(8,128)S(1)}, f32[288,128]{1,0:T(8,128)S(1)}, u32[]{:S(2)}, u32[]{:S(2)}) collective-permute-start(f32[288,128]{1,0:T(8,128)S(1)} %get-tuple-element.57), channel_id=1, source_target_pairs={{0,32},{1,33},{2,34},{3,35},{4,36},{5,37},{6,38},{7,39},{8,40},{9,... | collective-permute-start | bytes 442376 | tf_op jit(solution)/shard_map/ppermute | solution.py:27
  150.3 9.8 %collective-permute-start.24 = (f32[288,128]{1,0:T(8,128)S(1)}, f32[288,128]{1,0:T(8,128)S(1)}, u32[]{:S(2)}, u32[]{:S(2)}) collective-permute-start(f32[288,128]{1,0:T(8,128)S(1)} %get-tuple-element.58), channel_id=1, source_target_pairs={{0,48},{1,49},{2,50},{3,51},{4,52},{5,53},{6,54},{7,55},{8,56},{9,... | collective-permute-start | bytes 442376 | tf_op jit(solution)/shard_map/ppermute | solution.py:27
  160.2 9.0 %collective-permute-start.25 = (f32[32,128]{1,0:T(8,128)S(1)}, f32[32,128]{1,0:T(8,128)S(1)}, u32[]{:S(2)}, u32[]{:S(2)}) collective-permute-start(f32[32,128]{1,0:T(8,128)S(1)} %get-tuple-element.64), channel_id=1, source_target_pairs={{0,64},{1,5},{2,66},{3,7},{4,68},{5,9},{6,70},{7,11},{8,72},{9,13}... | collective-permute-start | bytes 49160 | tf_op jit(solution)/shard_map/ppermute | solution.py:27
  162.1 7.0 %collective-permute-start.26 = (f32[32,128]{1,0:T(8,128)S(1)}, f32[32,128]{1,0:T(8,128)S(1)}, u32[]{:S(2)}, u32[]{:S(2)}) collective-permute-start(f32[32,128]{1,0:T(8,128)S(1)} %get-tuple-element.64), channel_id=1, source_target_pairs={{0,128},{1,9},{2,130},{3,11},{4,132},{5,13},{6,134},{7,15},{8,136}... | collective-permute-start | bytes 49160 | tf_op jit(solution)/shard_map/ppermute | solution.py:27
  164.6 4.6 %collective-permute-start.27 = (f32[32,128]{1,0:T(8,128)S(1)}, f32[32,128]{1,0:T(8,128)S(1)}, u32[]{:S(2)}, u32[]{:S(2)}) collective-permute-start(f32[32,128]{1,0:T(8,128)S(1)} %get-tuple-element.64), channel_id=1, source_target_pairs={{0,192},{1,13},{2,194},{3,15},{4,196},{5,1},{6,198},{7,3},{8,200},... | collective-permute-start | bytes 49160 | tf_op jit(solution)/shard_map/ppermute | solution.py:27
  166.0 8.7 %collective-permute-start.31 = (f32[128,128]{1,0:T(8,128)S(1)}, f32[128,128]{1,0:T(8,128)S(1)}, u32[]{:S(2)}, u32[]{:S(2)}) collective-permute-start(f32[128,128]{1,0:T(8,128)S(1)} %get-tuple-element.61), channel_id=1, source_target_pairs={{0,2},{1,3},{2,130},{3,131},{4,6},{5,7},{6,134},{7,135},{8,10},{9,... | collective-permute-start | bytes 196616 | tf_op jit(solution)/shard_map/ppermute | solution.py:27
  168.5 6.2 %collective-permute-start.32 = (f32[128,128]{1,0:T(8,128)S(1)}, f32[128,128]{1,0:T(8,128)S(1)}, u32[]{:S(2)}, u32[]{:S(2)}) collective-permute-start(f32[128,128]{1,0:T(8,128)S(1)} %get-tuple-element.65.cross), channel_id=1, source_target_pairs={{3,66},{7,70},{11,74},{15,78},{19,82},{23,86},{27,90},{31,94},{35,... | collective-permute-start | bytes 196616 | tf_op jit(solution)/shard_map/ppermute | solution.py:27
  169.2 6.7 %collective-permute-start.28 = (f32[128,128]{1,0:T(8,128)S(1)}, f32[128,128]{1,0:T(8,128)S(1)}, u32[]{:S(2)}, u32[]{:S(2)}) collective-permute-start(f32[128,128]{1,0:T(8,128)S(1)} %pad_maximum_fusion.a), channel_id=1, source_target_pairs={{0,4},{1,65},{2,6},{3,67},{4,8},{5,69},{6,10},{7,71},{8,12},{9,73}... | collective-permute-start | bytes 196616 | tf_op jit(solution)/shard_map/ppermute | solution.py:27
  171.5 5.8 %collective-permute-start.29 = (f32[128,128]{1,0:T(8,128)S(1)}, f32[128,128]{1,0:T(8,128)S(1)}, u32[]{:S(2)}, u32[]{:S(2)}) collective-permute-start(f32[128,128]{1,0:T(8,128)S(1)} %pad_maximum_fusion.a), channel_id=1, source_target_pairs={{0,8},{1,129},{2,10},{3,131},{4,12},{5,133},{6,14},{7,135},{8,0},{... | collective-permute-start | bytes 196616 | tf_op jit(solution)/shard_map/ppermute | solution.py:27
  (7 other events, 76.5 us)

commit v3 on v2

--- a/solution.py
+++ b/solution.py
@@ -318,9 +318,10 @@
     )
     c0 = exchange(c0, first)
     c0 = middle((128, 40), *own, *c0, gate=c1[0])
+    ready = c0[0]
     c1 = exchange(c1, first)
     c0 = exchange(c0, second)
-    c = exchange(middle((96,), *c1, gate=gate), second)
+    c = exchange(middle((96,), *c1, gate=ready), second)
     c = exchange(sums_call(last_kernel, [(288, 128)] * 4, scalars, *c0, *c), along_z)
     c = (c[0] + c[1]) + (c[2] + c[3])
     own, pieces = c[:128], c[160:192]

time: 179 us -> 165 us (0.922)
  waiting for transfers between devices: 101 us -> 88.2 us
    ppermute x33, waiting for transfers between devices: 101 us -> 88.2 us  [move(): return lax.ppermute(values, AXES, pairs)]
  transfers between devices with their start and end apart: 33 -> 33, of which waited for: 11 -> 14; matrix products, arithmetic and copies ran while one was open for 2% -> 2% of each run, Pallas kernels for 5% -> 7%
where the time goes in v3:
time: 165 us
  waiting for transfers between devices  88.2 us (53%)
  starting transfers between devices  57.7 us (35%)
  Pallas kernels  14.5 us (9%)
  matrix products  3.28 us (2%)
    ppermute x33, waiting for transfers between devices, move(): return lax.ppermute(values, AXES, pairs)  88.2 us
    ppermute x33, starting transfers between devices, move(): return lax.ppermute(values, AXES, pairs)  57.7 us
    pallas_call x3, Pallas kernels, blocks_call(): pl.pallas_call(kernel, out_shape=outs, in_specs=[SMEM] + [VMEM] * len(ope...  9.8 us
    pallas_call x5, Pallas kernels, sums_call(): pl.pallas_call(kernel, out_shape=outs, in_specs=[SMEM] * len(head) + [VME...  4.74 us
  transfers between devices with their start and end apart: 33, of which 14 were waited for; matrix products, arithmetic and copies ran while one was open for 2% of the time, Pallas kernels for 7%

profile of v3, /device:TPU:32, one launch (start us, length us, event | category | flops | bytes accessed | tf_op | source)
XLA Modules:
  0.0 165.1 jit_solution(8508569048052011913)
XLA Ops:
  1.2 6.3 %collective-permute-start.3 = (bf16[1024,128]{1,0:T(8,128)(2,1)}, bf16[1024,128]{1,0:T(8,128)(2,1)S(1)}, u32[]{:S(2)}, u32[]{:S(2)}) collective-permute-start(bf16[1024,128]{1,0:T(8,128)(2,1)} %rest_0_.1), channel_id=1, source_target_pairs={{0,2},{1,3},{2,0},{3,1},{4,6},{5,7},{6,4},{7,5},{8,10},{9,11},{10,... | collective-permute-start | bytes 786440 | tf_op jit(solution)/shard_map/ppermute | solution.py:27
  7.6 2.5 %convolution_convert_fusion.1 = bf16[1024,128]{1,0:T(8,128)(2,1)} fusion(bf16[1024,512]{1,0:T(8,128)(2,1)} %vm.1, bf16[1024,512]{1,0:T(8,128)(2,1)} %km.1, pred[]{:T(512)S(6)} %eq.49, s32[128]{0:T(128)S(1)} %slice.18), kind=kOutput, calls=%fused_computation.1 | convolution fusion | flops 134938624 | bytes 2359809 | tf_op jit(solution)/shard_map/dot_general | solution.py:288
  11.0 5.9 %collective-permute-start.6 = (bf16[1024,384]{1,0:T(8,128)(2,1)S(1)}, bf16[1024,384]{1,0:T(8,128)(2,1)S(1)}, u32[]{:S(2)}, u32[]{:S(2)}) collective-permute-start(bf16[1024,384]{1,0:T(8,128)(2,1)S(1)} %convolution_convert_fusion), channel_id=1, source_target_pairs={{0,2},{1,3},{2,0},{3,1},{4,6},{5,7},{6,4},{7,5},{8,10},{9,11},{10,... | collective-permute-start | bytes 2359304 | tf_op jit(solution)/shard_map/ppermute | solution.py:27
  17.0 3.9 %shard_map.58 = (f32[2048,128]{1,0:T(8,128)S(1)}, f32[2048,128]{1,0:T(8,128)S(1)}, f32[2048,128]{1,0:T(8,128)S(1)}, f32[2048,128]{1,0:T(8,128)S(1)}) custom-call(s32[5]{0:T(128)S(1)} %stack.23.scalars, bf16[1024,512]{1,0:T(8,128)(2,1)S(1)} %copy-done, bf16[1024,512]{1,0:T(8,128)(2,1)S(1)} %collective-permute-done.ko, bf16[1024,512]{1,0:T(8,128)(2,1)S(1)} %copy-done.1, ...), custom_call_target="tpu_custom_call" | custom-call | tf_op jit(solution)/shard_map/pallas_call | solution.py:242
  20.9 1.6 collective-permute-start.7
  24.0 12.1 %collective-permute-done.5.rest_4_ = bf16[1024,128]{1,0:T(8,128)(2,1)} collective-permute-done((bf16[1024,128]{1,0:T(8,128)(2,1)}, bf16[1024,128]{1,0:T(8,128)(2,1)}, u32[]{:S(2)}, u32[]{:S(2)}) %collective-permute-start.5) | collective-permute-done | bytes 262176 | tf_op jit(solution)/shard_map/ppermute | solution.py:27
  36.1 2.9 %shard_map.59 = (f32[640,128]{1,0:T(8,128)S(1)}, f32[640,128]{1,0:T(8,128)S(1)}, f32[640,128]{1,0:T(8,128)S(1)}, f32[640,128]{1,0:T(8,128)S(1)}) custom-call(s32[5]{0:T(128)S(1)} %stack.23.scalars, bf16[1024,512]{1,0:T(8,128)(2,1)S(1)} %broadcast_select_fusion.2.nm, bf16[1024,512]{1,0:T(8,128)(2,1)S(1)} %broadcast_select_fusion.1.no, ...), custom_call_target="tpu_custom_call" | custom-call | tf_op jit(solution)/shard_map/pallas_call | solution.py:242
  39.1 1.6 collective-permute-start.10
  40.6 2.7 %collective-permute-start.11 = (f32[640,128]{1,0:T(8,128)S(1)}, f32[640,128]{1,0:T(8,128)S(1)}, u32[]{:S(2)}, u32[]{:S(2)}) collective-permute-start(f32[640,128]{1,0:T(8,128)S(1)} %get-tuple-element.43), channel_id=1, source_target_pairs={{0,128},{1,9},{2,130},{3,11},{4,132},{5,13},{6,134},{7,15},{8,136}... | collective-permute-start | bytes 983048 | tf_op jit(solution)/shard_map/ppermute | solution.py:27
  43.4 1.4 collective-permute-start.12
  44.8 20.4 %collective-permute-done.6.rest_0_ = bf16[1024,384]{1,0:T(8,128)(2,1)S(1)} collective-permute-done((bf16[1024,384]{1,0:T(8,128)(2,1)S(1)}, bf16[1024,384]{1,0:T(8,128)(2,1)S(1)}, u32[]{:S(2)}, u32[]{:S(2)}) %collective-permute-start.6) | collective-permute-done | bytes 786464 | tf_op jit(solution)/shard_map/ppermute | solution.py:27
  65.2 3.0 %collective-permute-start.8 = (f32[2048,128]{1,0:T(8,128)S(1)}, f32[2048,128]{1,0:T(8,128)S(1)}, u32[]{:S(2)}, u32[]{:S(2)}) collective-permute-start(f32[2048,128]{1,0:T(8,128)S(1)} %get-tuple-element.40), channel_id=1, source_target_pairs={{0,128},{1,9},{2,130},{3,11},{4,132},{5,13},{6,134},{7,15},{8,136}... | collective-permute-start | bytes 3145736 | tf_op jit(solution)/shard_map/ppermute | solution.py:27
  69.4 2.9 %shard_map.60 = (f32[1536,128]{1,0:T(8,128)S(1)}, f32[1536,128]{1,0:T(8,128)S(1)}, f32[1536,128]{1,0:T(8,128)S(1)}, f32[1536,128]{1,0:T(8,128)S(1)}) custom-call(s32[5]{0:T(128)S(1)} %stack.23.scalars, bf16[1024,512]{1,0:T(8,128)(2,1)S(1)} %broadcast_select_fusion.2.nm, bf16[1024,512]{1,0:T(8,128)(2,1)S(1)} %broadcast_select_fusion.1.no, ...), custom_call_target="tpu_custom_call" | custom-call | tf_op jit(solution)/shard_map/pallas_call | solution.py:242
  74.0 2.5 %collective-permute-start.18 = (f32[1536,128]{1,0:T(8,128)S(1)}, f32[1536,128]{1,0:T(8,128)S(1)}, u32[]{:S(2)}, u32[]{:S(2)}) collective-permute-start(f32[1536,128]{1,0:T(8,128)S(1)} %get-tuple-element.52), channel_id=1, source_target_pairs={{0,192},{1,13},{2,194},{3,15},{4,196},{5,1},{6,198},{7,3},{8,200},... | collective-permute-start | bytes 2359304 | tf_op jit(solution)/shard_map/ppermute | solution.py:27
  76.5 5.1 %collective-permute-done.8.refs_2_ = f32[2048,128]{1,0:T(8,128)S(1)} collective-permute-done((f32[2048,128]{1,0:T(8,128)S(1)}, f32[2048,128]{1,0:T(8,128)S(1)}, u32[]{:S(2)}, u32[]{:S(2)}) %collective-permute-start.8) | collective-permute-done | bytes 1048608 | tf_op jit(solution)/shard_map/ppermute | solution.py:27
  81.6 11.3 %collective-permute-done.9.refs_3_ = f32[2048,128]{1,0:T(8,128)S(1)} collective-permute-done((f32[2048,128]{1,0:T(8,128)S(1)}, f32[2048,128]{1,0:T(8,128)S(1)}, u32[]{:S(2)}, u32[]{:S(2)}) %collective-permute-start.9) | collective-permute-done | bytes 1048608 | tf_op jit(solution)/shard_map/ppermute | solution.py:27
  93.7 4.7 %collective-permute-done.17.refs_2_ = f32[1536,128]{1,0:T(8,128)S(1)} collective-permute-done((f32[1536,128]{1,0:T(8,128)S(1)}, f32[1536,128]{1,0:T(8,128)S(1)}, u32[]{:S(2)}, u32[]{:S(2)}) %collective-permute-start.17) | collective-permute-done | bytes 786464 | tf_op jit(solution)/shard_map/ppermute | solution.py:27
  98.4 11.4 %collective-permute-done.18.refs_3_ = f32[1536,128]{1,0:T(8,128)S(1)} collective-permute-done((f32[1536,128]{1,0:T(8,128)S(1)}, f32[1536,128]{1,0:T(8,128)S(1)}, u32[]{:S(2)}, u32[]{:S(2)}) %collective-permute-start.18) | collective-permute-done | bytes 786464 | tf_op jit(solution)/shard_map/ppermute | solution.py:27
  110.5 1.7 %collective-permute-start.19 = (f32[384,128]{1,0:T(8,128)S(1)}, f32[384,128]{1,0:T(8,128)S(1)}, u32[]{:S(2)}, u32[]{:S(2)}) collective-permute-start(f32[384,128]{1,0:T(8,128)S(1)} %get-tuple-element.54), channel_id=1, source_target_pairs={{0,4},{1,65},{2,6},{3,67},{4,8},{5,69},{6,10},{7,71},{8,12},{9,73}... | collective-permute-start | bytes 589832 | tf_op jit(solution)/shard_map/ppermute | solution.py:27
  112.1 1.6 collective-permute-start.13
  113.7 1.5 collective-permute-start.14
  115.3 2.4 %collective-permute-start.15 = (f32[672,128]{1,0:T(8,128)S(1)}, f32[672,128]{1,0:T(8,128)S(1)}, u32[]{:S(2)}, u32[]{:S(2)}) collective-permute-start(f32[672,128]{1,0:T(8,128)S(1)} %get-tuple-element.48), channel_id=1, source_target_pairs={{0,12},{1,193},{2,14},{3,195},{4,0},{5,197},{6,2},{7,199},{8,4},{9... | collective-permute-start | bytes 1032200 | tf_op jit(solution)/shard_map/ppermute | solution.py:27
  118.3 1.7 %collective-permute-start.21 = (f32[384,128]{1,0:T(8,128)S(1)}, f32[384,128]{1,0:T(8,128)S(1)}, u32[]{:S(2)}, u32[]{:S(2)}) collective-permute-start(f32[384,128]{1,0:T(8,128)S(1)} %get-tuple-element.56), channel_id=1, source_target_pairs={{0,12},{1,193},{2,14},{3,195},{4,0},{5,197},{6,2},{7,199},{8,4},{9... | collective-permute-start | bytes 589832 | tf_op jit(solution)/shard_map/ppermute | solution.py:27
  120.0 8.2 %collective-permute-done.20.g = f32[384,128]{1,0:T(8,128)S(1)} collective-permute-done((f32[384,128]{1,0:T(8,128)S(1)}, f32[384,128]{1,0:T(8,128)S(1)}, u32[]{:S(2)}, u32[]{:S(2)}) %collective-permute-start.20) | collective-permute-done | bytes 196640 | tf_op jit(solution)/shard_map/ppermute | solution.py:27
  130.2 5.3 %collective-permute-start.23 = (f32[288,128]{1,0:T(8,128)S(1)}, f32[288,128]{1,0:T(8,128)S(1)}, u32[]{:S(2)}, u32[]{:S(2)}) collective-permute-start(f32[288,128]{1,0:T(8,128)S(1)} %get-tuple-element.59), channel_id=1, source_target_pairs={{0,32},{1,33},{2,34},{3,35},{4,36},{5,37},{6,38},{7,39},{8,40},{9,... | collective-permute-start | bytes 442376 | tf_op jit(solution)/shard_map/ppermute | solution.py:27
  135.5 2.4 %collective-permute-done.22 = f32[288,128]{1,0:T(8,128)S(1)} collective-permute-done((f32[288,128]{1,0:T(8,128)S(1)}, f32[288,128]{1,0:T(8,128)S(1)}, u32[]{:S(2)}, u32[]{:S(2)}) %collective-permute-start.22) | collective-permute-done | bytes 147488 | tf_op jit(solution)/shard_map/ppermute | solution.py:27
  137.9 4.5 %collective-permute-done.23 = f32[288,128]{1,0:T(8,128)S(1)} collective-permute-done((f32[288,128]{1,0:T(8,128)S(1)}, f32[288,128]{1,0:T(8,128)S(1)}, u32[]{:S(2)}, u32[]{:S(2)}) %collective-permute-start.23) | collective-permute-done | bytes 147488 | tf_op jit(solution)/shard_map/ppermute | solution.py:27
  142.3 3.2 %collective-permute-done.24 = f32[288,128]{1,0:T(8,128)S(1)} collective-permute-done((f32[288,128]{1,0:T(8,128)S(1)}, f32[288,128]{1,0:T(8,128)S(1)}, u32[]{:S(2)}, u32[]{:S(2)}) %collective-permute-start.24) | collective-permute-done | bytes 147488 | tf_op jit(solution)/shard_map/ppermute | solution.py:27
  145.5 2.0 %collective-permute-start.25 = (f32[32,128]{1,0:T(8,128)S(1)}, f32[32,128]{1,0:T(8,128)S(1)}, u32[]{:S(2)}, u32[]{:S(2)}) collective-permute-start(f32[32,128]{1,0:T(8,128)S(1)} %get-tuple-element.66), channel_id=1, source_target_pairs={{0,64},{1,5},{2,66},{3,7},{4,68},{5,9},{6,70},{7,11},{8,72},{9,13}... | collective-permute-start | bytes 49160 | tf_op jit(solution)/shard_map/ppermute | solution.py:27
  147.5 2.4 %collective-permute-start.26 = (f32[32,128]{1,0:T(8,128)S(1)}, f32[32,128]{1,0:T(8,128)S(1)}, u32[]{:S(2)}, u32[]{:S(2)}) collective-permute-start(f32[32,128]{1,0:T(8,128)S(1)} %get-tuple-element.66), channel_id=1, source_target_pairs={{0,128},{1,9},{2,130},{3,11},{4,132},{5,13},{6,134},{7,15},{8,136}... | collective-permute-start | bytes 49160 | tf_op jit(solution)/shard_map/ppermute | solution.py:27
  151.3 3.4 %collective-permute-start.31 = (f32[128,128]{1,0:T(8,128)S(1)}, f32[128,128]{1,0:T(8,128)S(1)}, u32[]{:S(2)}, u32[]{:S(2)}) collective-permute-start(f32[128,128]{1,0:T(8,128)S(1)} %get-tuple-element.63), channel_id=1, source_target_pairs={{0,2},{1,3},{2,130},{3,131},{4,6},{5,7},{6,134},{7,135},{8,10},{9,... | collective-permute-start | bytes 196616 | tf_op jit(solution)/shard_map/ppermute | solution.py:27
  156.6 2.9 %collective-permute-start.29 = (f32[128,128]{1,0:T(8,128)S(1)}, f32[128,128]{1,0:T(8,128)S(1)}, u32[]{:S(2)}, u32[]{:S(2)}) collective-permute-start(f32[128,128]{1,0:T(8,128)S(1)} %pad_maximum_fusion.a), channel_id=1, source_target_pairs={{0,8},{1,129},{2,10},{3,131},{4,12},{5,133},{6,14},{7,135},{8,0},{... | collective-permute-start | bytes 196616 | tf_op jit(solution)/shard_map/ppermute | solution.py:27
  (62 shorter events, 18.9 us)
Async XLA Ops:
  0.6 10.4 %collective-permute-start = (bf16[1024,512]{1,0:T(8,128)(2,1)}, bf16[1024,512]{1,0:T(8,128)(2,1)S(1)}, u32[]{:S(2)}, u32[]{:S(2)}) collective-permute-start(bf16[1024,512]{1,0:T(8,128)(2,1)} %km.1), channel_id=1, source_target_pairs={{0,1},{1,0},{2,3},{3,2},{4,5},{5,4},{6,7},{7,6},{8,9},{9,8},{10,11... | collective-permute-start | bytes 3145736 | tf_op jit(solution)/shard_map/ppermute | solution.py:27
  0.7 16.3 %collective-permute-start.1 = (bf16[1024,512]{1,0:T(8,128)(2,1)}, bf16[1024,512]{1,0:T(8,128)(2,1)}, u32[]{:S(2)}, u32[]{:S(2)}) collective-permute-start(bf16[1024,512]{1,0:T(8,128)(2,1)} %vm.1), channel_id=1, source_target_pairs={{0,1},{1,0},{2,3},{3,2},{4,5},{5,4},{6,7},{7,6},{8,9},{9,8},{10,11... | collective-permute-start | bytes 3145736 | tf_op jit(solution)/shard_map/ppermute | solution.py:27
  1.2 22.6 %collective-permute-start.3 = (bf16[1024,128]{1,0:T(8,128)(2,1)}, bf16[1024,128]{1,0:T(8,128)(2,1)S(1)}, u32[]{:S(2)}, u32[]{:S(2)}) collective-permute-start(bf16[1024,128]{1,0:T(8,128)(2,1)} %rest_0_.1), channel_id=1, source_target_pairs={{0,2},{1,3},{2,0},{3,1},{4,6},{5,7},{6,4},{7,5},{8,10},{9,11},{10,... | collective-permute-start | bytes 786440 | tf_op jit(solution)/shard_map/ppermute | solution.py:27
  7.5 28.6 %collective-permute-start.2 = (bf16[1024,128]{1,0:T(8,128)(2,1)}, bf16[1024,128]{1,0:T(8,128)(2,1)}, u32[]{:S(2)}, u32[]{:S(2)}) collective-permute-start(bf16[1024,128]{1,0:T(8,128)(2,1)} %rest_0_.1), channel_id=1, source_target_pairs={{0,1},{1,0},{2,3},{3,2},{4,5},{5,4},{6,7},{7,6},{8,9},{9,8},{10,11... | collective-permute-start | bytes 786440 | tf_op jit(solution)/shard_map/ppermute | solution.py:27
  10.1 26.0 %collective-permute-start.5 = (bf16[1024,128]{1,0:T(8,128)(2,1)}, bf16[1024,128]{1,0:T(8,128)(2,1)}, u32[]{:S(2)}, u32[]{:S(2)}) collective-permute-start(bf16[1024,128]{1,0:T(8,128)(2,1)} %convolution_convert_fusion.1), channel_id=1, source_target_pairs={{0,2},{1,3},{2,0},{3,1},{4,6},{5,7},{6,4},{7,5},{8,10},{9,11},{10,... | collective-permute-start | bytes 786440 | tf_op jit(solution)/shard_map/ppermute | solution.py:27
  11.0 54.2 %collective-permute-start.6 = (bf16[1024,384]{1,0:T(8,128)(2,1)S(1)}, bf16[1024,384]{1,0:T(8,128)(2,1)S(1)}, u32[]{:S(2)}, u32[]{:S(2)}) collective-permute-start(bf16[1024,384]{1,0:T(8,128)(2,1)S(1)} %convolution_convert_fusion), channel_id=1, source_target_pairs={{0,2},{1,3},{2,0},{3,1},{4,6},{5,7},{6,4},{7,5},{8,10},{9,11},{10,... | collective-permute-start | bytes 2359304 | tf_op jit(solution)/shard_map/ppermute | solution.py:27
  20.9 53.1 %collective-permute-start.7 = (f32[2048,128]{1,0:T(8,128)S(1)}, f32[2048,128]{1,0:T(8,128)S(1)}, u32[]{:S(2)}, u32[]{:S(2)}) collective-permute-start(f32[2048,128]{1,0:T(8,128)S(1)} %get-tuple-element.39), channel_id=1, source_target_pairs={{0,64},{1,5},{2,66},{3,7},{4,68},{5,9},{6,70},{7,11},{8,72},{9,13}... | collective-permute-start | bytes 3145736 | tf_op jit(solution)/shard_map/ppermute | solution.py:27
  23.8 12.3 %collective-permute-start.4 = (bf16[1024,128]{1,0:T(8,128)(2,1)S(1)}, bf16[1024,128]{1,0:T(8,128)(2,1)S(1)}, u32[]{:S(2)}, u32[]{:S(2)}) collective-permute-start(bf16[1024,128]{1,0:T(8,128)(2,1)S(1)} %collective-permute-done.3.rest_2_), channel_id=1, source_target_pairs={{0,1},{1,0},{2,3},{3,2},{4,5},{5,4},{6,7},{7,6},{8,9},{9,8},{10,11... | collective-permute-start | bytes 786440 | tf_op jit(solution)/shard_map/ppermute | solution.py:27
  39.1 29.2 %collective-permute-start.10 = (f32[640,128]{1,0:T(8,128)S(1)}, f32[640,128]{1,0:T(8,128)S(1)}, u32[]{:S(2)}, u32[]{:S(2)}) collective-permute-start(f32[640,128]{1,0:T(8,128)S(1)} %get-tuple-element.42), channel_id=1, source_target_pairs={{0,64},{1,5},{2,66},{3,7},{4,68},{5,9},{6,70},{7,11},{8,72},{9,13}... | collective-permute-start | bytes 983048 | tf_op jit(solution)/shard_map/ppermute | solution.py:27
  40.6 31.7 %collective-permute-start.11 = (f32[640,128]{1,0:T(8,128)S(1)}, f32[640,128]{1,0:T(8,128)S(1)}, u32[]{:S(2)}, u32[]{:S(2)}) collective-permute-start(f32[640,128]{1,0:T(8,128)S(1)} %get-tuple-element.43), channel_id=1, source_target_pairs={{0,128},{1,9},{2,130},{3,11},{4,132},{5,13},{6,134},{7,15},{8,136}... | collective-permute-start | bytes 983048 | tf_op jit(solution)/shard_map/ppermute | solution.py:27
  43.4 29.9 %collective-permute-start.12 = (f32[640,128]{1,0:T(8,128)S(1)}, f32[640,128]{1,0:T(8,128)S(1)}, u32[]{:S(2)}, u32[]{:S(2)}) collective-permute-start(f32[640,128]{1,0:T(8,128)S(1)} %get-tuple-element.44), channel_id=1, source_target_pairs={{0,192},{1,13},{2,194},{3,15},{4,196},{5,1},{6,198},{7,3},{8,200},... | collective-permute-start | bytes 983048 | tf_op jit(solution)/shard_map/ppermute | solution.py:27
  65.2 16.4 %collective-permute-start.8 = (f32[2048,128]{1,0:T(8,128)S(1)}, f32[2048,128]{1,0:T(8,128)S(1)}, u32[]{:S(2)}, u32[]{:S(2)}) collective-permute-start(f32[2048,128]{1,0:T(8,128)S(1)} %get-tuple-element.40), channel_id=1, source_target_pairs={{0,128},{1,9},{2,130},{3,11},{4,132},{5,13},{6,134},{7,15},{8,136}... | collective-permute-start | bytes 3145736 | tf_op jit(solution)/shard_map/ppermute | solution.py:27
  68.2 24.6 %collective-permute-start.9 = (f32[2048,128]{1,0:T(8,128)S(1)}, f32[2048,128]{1,0:T(8,128)S(1)}, u32[]{:S(2)}, u32[]{:S(2)}) collective-permute-start(f32[2048,128]{1,0:T(8,128)S(1)} %get-tuple-element.41), channel_id=1, source_target_pairs={{0,192},{1,13},{2,194},{3,15},{4,196},{5,1},{6,198},{7,3},{8,200},... | collective-permute-start | bytes 3145736 | tf_op jit(solution)/shard_map/ppermute | solution.py:27
  72.3 21.4 %collective-permute-start.16 = (f32[1536,128]{1,0:T(8,128)S(1)}, f32[1536,128]{1,0:T(8,128)S(1)}, u32[]{:S(2)}, u32[]{:S(2)}) collective-permute-start(f32[1536,128]{1,0:T(8,128)S(1)} %get-tuple-element.50), channel_id=1, source_target_pairs={{0,64},{1,5},{2,66},{3,7},{4,68},{5,9},{6,70},{7,11},{8,72},{9,13}... | collective-permute-start | bytes 2359304 | tf_op jit(solution)/shard_map/ppermute | solution.py:27
  73.3 25.1 %collective-permute-start.17 = (f32[1536,128]{1,0:T(8,128)S(1)}, f32[1536,128]{1,0:T(8,128)S(1)}, u32[]{:S(2)}, u32[]{:S(2)}) collective-permute-start(f32[1536,128]{1,0:T(8,128)S(1)} %get-tuple-element.51), channel_id=1, source_target_pairs={{0,128},{1,9},{2,130},{3,11},{4,132},{5,13},{6,134},{7,15},{8,136}... | collective-permute-start | bytes 2359304 | tf_op jit(solution)/shard_map/ppermute | solution.py:27
  74.0 35.7 %collective-permute-start.18 = (f32[1536,128]{1,0:T(8,128)S(1)}, f32[1536,128]{1,0:T(8,128)S(1)}, u32[]{:S(2)}, u32[]{:S(2)}) collective-permute-start(f32[1536,128]{1,0:T(8,128)S(1)} %get-tuple-element.52), channel_id=1, source_target_pairs={{0,192},{1,13},{2,194},{3,15},{4,196},{5,1},{6,198},{7,3},{8,200},... | collective-permute-start | bytes 2359304 | tf_op jit(solution)/shard_map/ppermute | solution.py:27
  110.5 7.8 %collective-permute-start.19 = (f32[384,128]{1,0:T(8,128)S(1)}, f32[384,128]{1,0:T(8,128)S(1)}, u32[]{:S(2)}, u32[]{:S(2)}) collective-permute-start(f32[384,128]{1,0:T(8,128)S(1)} %get-tuple-element.54), channel_id=1, source_target_pairs={{0,4},{1,65},{2,6},{3,67},{4,8},{5,69},{6,10},{7,71},{8,12},{9,73}... | collective-permute-start | bytes 589832 | tf_op jit(solution)/shard_map/ppermute | solution.py:27
  112.1 17.3 %collective-permute-start.13 = (f32[672,128]{1,0:T(8,128)S(1)}, f32[672,128]{1,0:T(8,128)S(1)}, u32[]{:S(2)}, u32[]{:S(2)}) collective-permute-start(f32[672,128]{1,0:T(8,128)S(1)} %get-tuple-element.46), channel_id=1, source_target_pairs={{0,4},{1,65},{2,6},{3,67},{4,8},{5,69},{6,10},{7,71},{8,12},{9,73}... | collective-permute-start | bytes 1032200 | tf_op jit(solution)/shard_map/ppermute | solution.py:27
  113.7 15.7 %collective-permute-start.14 = (f32[672,128]{1,0:T(8,128)S(1)}, f32[672,128]{1,0:T(8,128)S(1)}, u32[]{:S(2)}, u32[]{:S(2)}) collective-permute-start(f32[672,128]{1,0:T(8,128)S(1)} %get-tuple-element.47), channel_id=1, source_target_pairs={{0,8},{1,129},{2,10},{3,131},{4,12},{5,133},{6,14},{7,135},{8,0},{... | collective-permute-start | bytes 1032200 | tf_op jit(solution)/shard_map/ppermute | solution.py:27
  115.3 14.2 %collective-permute-start.15 = (f32[672,128]{1,0:T(8,128)S(1)}, f32[672,128]{1,0:T(8,128)S(1)}, u32[]{:S(2)}, u32[]{:S(2)}) collective-permute-start(f32[672,128]{1,0:T(8,128)S(1)} %get-tuple-element.48), channel_id=1, source_target_pairs={{0,12},{1,193},{2,14},{3,195},{4,0},{5,197},{6,2},{7,199},{8,4},{9... | collective-permute-start | bytes 1032200 | tf_op jit(solution)/shard_map/ppermute | solution.py:27
  117.7 10.5 %collective-permute-start.20 = (f32[384,128]{1,0:T(8,128)S(1)}, f32[384,128]{1,0:T(8,128)S(1)}, u32[]{:S(2)}, u32[]{:S(2)}) collective-permute-start(f32[384,128]{1,0:T(8,128)S(1)} %get-tuple-element.55), channel_id=1, source_target_pairs={{0,8},{1,129},{2,10},{3,131},{4,12},{5,133},{6,14},{7,135},{8,0},{... | collective-permute-start | bytes 589832 | tf_op jit(solution)/shard_map/ppermute | solution.py:27
  118.3 11.1 %collective-permute-start.21 = (f32[384,128]{1,0:T(8,128)S(1)}, f32[384,128]{1,0:T(8,128)S(1)}, u32[]{:S(2)}, u32[]{:S(2)}) collective-permute-start(f32[384,128]{1,0:T(8,128)S(1)} %get-tuple-element.56), channel_id=1, source_target_pairs={{0,12},{1,193},{2,14},{3,195},{4,0},{5,197},{6,2},{7,199},{8,4},{9... | collective-permute-start | bytes 589832 | tf_op jit(solution)/shard_map/ppermute | solution.py:27
  130.1 7.8 %collective-permute-start.22 = (f32[288,128]{1,0:T(8,128)S(1)}, f32[288,128]{1,0:T(8,128)S(1)}, u32[]{:S(2)}, u32[]{:S(2)}) collective-permute-start(f32[288,128]{1,0:T(8,128)S(1)} %get-tuple-element.58), channel_id=1, source_target_pairs={{0,16},{1,17},{2,18},{3,19},{4,20},{5,21},{6,22},{7,23},{8,24},{9,... | collective-permute-start | bytes 442376 | tf_op jit(solution)/shard_map/ppermute | solution.py:27
  130.2 12.1 %collective-permute-start.23 = (f32[288,128]{1,0:T(8,128)S(1)}, f32[288,128]{1,0:T(8,128)S(1)}, u32[]{:S(2)}, u32[]{:S(2)}) collective-permute-start(f32[288,128]{1,0:T(8,128)S(1)} %get-tuple-element.59), channel_id=1, source_target_pairs={{0,32},{1,33},{2,34},{3,35},{4,36},{5,37},{6,38},{7,39},{8,40},{9,... | collective-permute-start | bytes 442376 | tf_op jit(solution)/shard_map/ppermute | solution.py:27
  135.5 10.0 %collective-permute-start.24 = (f32[288,128]{1,0:T(8,128)S(1)}, f32[288,128]{1,0:T(8,128)S(1)}, u32[]{:S(2)}, u32[]{:S(2)}) collective-permute-start(f32[288,128]{1,0:T(8,128)S(1)} %get-tuple-element.60), channel_id=1, source_target_pairs={{0,48},{1,49},{2,50},{3,51},{4,52},{5,53},{6,54},{7,55},{8,56},{9,... | collective-permute-start | bytes 442376 | tf_op jit(solution)/shard_map/ppermute | solution.py:27
  145.5 9.8 %collective-permute-start.25 = (f32[32,128]{1,0:T(8,128)S(1)}, f32[32,128]{1,0:T(8,128)S(1)}, u32[]{:S(2)}, u32[]{:S(2)}) collective-permute-start(f32[32,128]{1,0:T(8,128)S(1)} %get-tuple-element.66), channel_id=1, source_target_pairs={{0,64},{1,5},{2,66},{3,7},{4,68},{5,9},{6,70},{7,11},{8,72},{9,13}... | collective-permute-start | bytes 49160 | tf_op jit(solution)/shard_map/ppermute | solution.py:27
  147.5 7.9 %collective-permute-start.26 = (f32[32,128]{1,0:T(8,128)S(1)}, f32[32,128]{1,0:T(8,128)S(1)}, u32[]{:S(2)}, u32[]{:S(2)}) collective-permute-start(f32[32,128]{1,0:T(8,128)S(1)} %get-tuple-element.66), channel_id=1, source_target_pairs={{0,128},{1,9},{2,130},{3,11},{4,132},{5,13},{6,134},{7,15},{8,136}... | collective-permute-start | bytes 49160 | tf_op jit(solution)/shard_map/ppermute | solution.py:27
  149.9 5.5 %collective-permute-start.27 = (f32[32,128]{1,0:T(8,128)S(1)}, f32[32,128]{1,0:T(8,128)S(1)}, u32[]{:S(2)}, u32[]{:S(2)}) collective-permute-start(f32[32,128]{1,0:T(8,128)S(1)} %get-tuple-element.66), channel_id=1, source_target_pairs={{0,192},{1,13},{2,194},{3,15},{4,196},{5,1},{6,198},{7,3},{8,200},... | collective-permute-start | bytes 49160 | tf_op jit(solution)/shard_map/ppermute | solution.py:27
  151.3 8.7 %collective-permute-start.31 = (f32[128,128]{1,0:T(8,128)S(1)}, f32[128,128]{1,0:T(8,128)S(1)}, u32[]{:S(2)}, u32[]{:S(2)}) collective-permute-start(f32[128,128]{1,0:T(8,128)S(1)} %get-tuple-element.63), channel_id=1, source_target_pairs={{0,2},{1,3},{2,130},{3,131},{4,6},{5,7},{6,134},{7,135},{8,10},{9,... | collective-permute-start | bytes 196616 | tf_op jit(solution)/shard_map/ppermute | solution.py:27
  154.7 5.3 %collective-permute-start.32 = (f32[128,128]{1,0:T(8,128)S(1)}, f32[128,128]{1,0:T(8,128)S(1)}, u32[]{:S(2)}, u32[]{:S(2)}) collective-permute-start(f32[128,128]{1,0:T(8,128)S(1)} %get-tuple-element.67.cross), channel_id=1, source_target_pairs={{3,66},{7,70},{11,74},{15,78},{19,82},{23,86},{27,90},{31,94},{35,... | collective-permute-start | bytes 196616 | tf_op jit(solution)/shard_map/ppermute | solution.py:27
  155.4 5.8 %collective-permute-start.28 = (f32[128,128]{1,0:T(8,128)S(1)}, f32[128,128]{1,0:T(8,128)S(1)}, u32[]{:S(2)}, u32[]{:S(2)}) collective-permute-start(f32[128,128]{1,0:T(8,128)S(1)} %pad_maximum_fusion.a), channel_id=1, source_target_pairs={{0,4},{1,65},{2,6},{3,67},{4,8},{5,69},{6,10},{7,71},{8,12},{9,73}... | collective-permute-start | bytes 196616 | tf_op jit(solution)/shard_map/ppermute | solution.py:27
  156.6 5.8 %collective-permute-start.29 = (f32[128,128]{1,0:T(8,128)S(1)}, f32[128,128]{1,0:T(8,128)S(1)}, u32[]{:S(2)}, u32[]{:S(2)}) collective-permute-start(f32[128,128]{1,0:T(8,128)S(1)} %pad_maximum_fusion.a), channel_id=1, source_target_pairs={{0,8},{1,129},{2,10},{3,131},{4,12},{5,133},{6,14},{7,135},{8,0},{... | collective-permute-start | bytes 196616 | tf_op jit(solution)/shard_map/ppermute | solution.py:27
  (4 other events, 22.0 us)
